TPU v7x, 32 devices: a whole 2x2x4 slice. The times are simulated.
32 devices in a mesh: seq: 8 (over z, core), batch: 4 (over y, x).
Axes of the slice: x: 2, y: 2, z: 4, core: 2. Of those that a mesh axis runs over, the one named last changes fastest.
Arguments:
- block_input: bfloat16 [128, 1024, 512], P('batch', 'seq'), may hold values from -6 to 6
- window_lengths: int32 [128], P('batch'), may hold values from 256 to 1024, as said below
- conv_weight: bfloat16 [9, 512, 512], replicated, may hold values from -0.09375 to 0.09375
- conv_bias: float32 [512], replicated, may hold values from -3 to 3
- norm1_gain: float32 [512], replicated, may hold values from 0.1 to 1.9
- norm1_bias: float32 [512], replicated, may hold values from -3 to 3
- up_weight: bfloat16 [512, 2048], replicated, may hold values from -0.25 to 0.25
- up_bias: float32 [2048], replicated, may hold values from -3 to 3
- down_weight: bfloat16 [2048, 512], replicated, may hold values from -0.125 to 0.125
- down_bias: float32 [512], replicated, may hold values from -3 to 3
- norm2_gain: float32 [512], replicated, may hold values from 0.1 to 1.9
- norm2_bias: float32 [512], replicated, may hold values from -3 to 3
- out_cotangent: bfloat16 [128, 1024, 512], P('batch', 'seq'), may hold values from -6 to 6
Outputs:
- block_output: bfloat16 [128, 1024, 512], P('batch', 'seq')
- input_grad: bfloat16 [128, 1024, 512], P('batch', 'seq')
- conv_weight_grad: float32 [9, 512, 512], replicated
- conv_bias_grad: float32 [512], replicated
- norm1_gain_grad: float32 [512], replicated
- norm1_bias_grad: float32 [512], replicated
- up_weight_grad: float32 [512, 2048], replicated
- up_bias_grad: float32 [2048], replicated
- down_weight_grad: float32 [2048, 512], replicated
- down_bias_grad: float32 [512], replicated
- norm2_gain_grad: float32 [512], replicated
- norm2_bias_grad: float32 [512], replicated
Inputs may be any that keep to these rules, and one draw needn't show every extreme that they name: `window_lengths`: each window's length is 256, 512 or 1024; among each 32 consecutive windows at least one has length 1024.
All inputs are finite; a program needn't handle non-finite values.
Results may differ from a plain program's by a relative error of at most 0.0075.
Values may be sent and summed in bfloat16 or wider, within the bound.
A program may use at most 320 MiB of HBM per device.

v0:
```python
import math

import jax
import jax.numpy as jnp
from jax import lax
from jax.sharding import PartitionSpec as P

KERNEL = 9
DILATION = 32


def passed_along(shard, axis, by):
    size = lax.axis_size(axis)
    pairs = [(i, i + by) for i in range(size) if 0 <= i + by < size]
    return lax.ppermute(shard, axis, pairs)


def normalize(values, gain, shift):
    center = jnp.mean(values, axis=-1, keepdims=True)
    centered = values - center
    inverse = lax.rsqrt(jnp.mean(centered * centered, axis=-1, keepdims=True) + 1e-05)
    normed = centered * inverse
    return (normed * gain + shift, normed, inverse)


def normalize_back(upstream, normed, inverse, gain):
    inner = upstream * gain
    return inverse * (
        inner
        - jnp.mean(inner, axis=-1, keepdims=True)
        - normed * jnp.mean(inner * normed, axis=-1, keepdims=True)
    )


def gelu_slope(values):
    cumulative = 0.5 * (1.0 + lax.erf(values * (1.0 / math.sqrt(2.0))))
    density = jnp.exp(-0.5 * values * values) * (1.0 / math.sqrt(2.0 * math.pi))
    return cumulative + values * density


def taps_apply(source, weight, bias, base_row, count):
    result = jnp.zeros(source.shape[:1] + (count,) + source.shape[2:], jnp.float32) + bias
    for tap_index in range(weight.shape[0]):
        begin = base_row + tap_index
        result = result + jnp.einsum(
            "wtpd,de->wtpe",
            source[:, begin : begin + count],
            weight[tap_index],
            preferred_element_type=jnp.float32,
        )
    return result


def taps_grads(source, grad_low, weight, base_row, count):
    weight_parts = []
    source_grad = jnp.zeros(source.shape, jnp.float32)
    for tap_index in range(weight.shape[0]):
        begin = base_row + tap_index
        weight_parts.append(
            jnp.einsum(
                "wtpd,wtpe->de",
                source[:, begin : begin + count],
                grad_low,
                preferred_element_type=jnp.float32,
            )
        )
        source_grad = source_grad.at[:, begin : begin + count].add(
            jnp.einsum(
                "wtpe,de->wtpd", grad_low, weight[tap_index], preferred_element_type=jnp.float32
            )
        )
    return (jnp.stack(weight_parts), source_grad)


def branch_forward(source, base_row, count, conv_weight, conv_bias, norm_gain, norm_shift):
    pre_conv = taps_apply(source, conv_weight, conv_bias, base_row, count)
    activated = jax.nn.gelu(pre_conv, approximate=False)
    branch_out, normed, inverse = normalize(activated, norm_gain, norm_shift)
    return (branch_out.astype(jnp.bfloat16), (pre_conv, normed, inverse))


def branch_backward(source, base_row, count, grad_low, saved, conv_weight, norm_gain):
    pre_conv, normed, inverse = saved
    upstream = grad_low.astype(jnp.float32)
    gain_grad = jnp.sum(upstream * normed, axis=(0, 1, 2))
    shift_grad = jnp.sum(upstream, axis=(0, 1, 2))
    act_grad = normalize_back(upstream, normed, inverse, norm_gain)
    pre_low = (act_grad * gelu_slope(pre_conv)).astype(jnp.bfloat16)
    bias_grad = jnp.sum(pre_low.astype(jnp.float32), axis=(0, 1, 2))
    weight_grad, source_grad = taps_grads(source, pre_low, conv_weight, base_row, count)
    return ((weight_grad, bias_grad, gain_grad, shift_grad), source_grad)


def per_device(
    block_input,
    window_lengths,
    conv_weight,
    conv_bias,
    norm1_gain,
    norm1_bias,
    up_weight,
    up_bias,
    down_weight,
    down_bias,
    norm2_gain,
    norm2_bias,
    out_cotangent,
):
    windows, rows_here, width = block_input.shape
    groups_here = rows_here // DILATION
    half_taps = KERNEL // 2
    position = lax.axis_index("seq") * rows_here + jnp.arange(rows_here, dtype=jnp.int32)
    keep_mask = (position[None, :] < window_lengths[:, None]).astype(jnp.float32)[:, :, None]
    start_rows = keep_mask * block_input.astype(jnp.float32)
    start_low = start_rows.astype(jnp.bfloat16)
    reach = DILATION * half_taps
    depth = -(-reach // rows_here)
    pieces = []
    for offset in range(depth, -depth - 1, -1):
        if offset == 0:
            pieces.append(start_low)
        else:
            pieces.append(passed_along(start_low, "seq", offset))
    extended = jnp.concatenate(pieces, axis=1)
    source = extended.reshape(windows, (2 * depth + 1) * groups_here, DILATION, width)
    base_row = (depth * rows_here - reach) // DILATION
    branch_low, saved = branch_forward(
        source, base_row, groups_here, conv_weight, conv_bias, norm1_gain, norm1_bias
    )
    branch_rows = branch_low.reshape(windows, rows_here, width)
    middle = start_rows + branch_rows.astype(jnp.float32)
    middle_low = middle.astype(jnp.bfloat16).reshape(-1, width)
    upper = jnp.dot(middle_low, up_weight, preferred_element_type=jnp.float32) + up_bias
    hidden_low = jax.nn.gelu(upper, approximate=False).astype(jnp.bfloat16)
    lower = jnp.dot(hidden_low, down_weight, preferred_element_type=jnp.float32) + down_bias
    normed_out, normed_two, inverse_two = normalize(lower, norm2_gain, norm2_bias)
    block_output = (keep_mask * (middle + normed_out.reshape(middle.shape))).astype(jnp.bfloat16)
    incoming = (keep_mask * out_cotangent.astype(jnp.float32)).reshape(-1, width)
    gain_two_grad = jnp.sum(incoming * normed_two, axis=0)
    shift_two_grad = jnp.sum(incoming, axis=0)
    lower_low = normalize_back(incoming, normed_two, inverse_two, norm2_gain).astype(jnp.bfloat16)
    down_bias_grad = jnp.sum(lower_low.astype(jnp.float32), axis=0)
    down_grad = jnp.einsum("tf,td->fd", hidden_low, lower_low, preferred_element_type=jnp.float32)
    hidden_grad = jnp.einsum(
        "td,fd->tf", lower_low, down_weight, preferred_element_type=jnp.float32
    )
    upper_low = (hidden_grad * gelu_slope(upper)).astype(jnp.bfloat16)
    up_bias_grad = jnp.sum(upper_low.astype(jnp.float32), axis=0)
    up_grad = jnp.einsum("td,tf->df", middle_low, upper_low, preferred_element_type=jnp.float32)
    middle_grad = incoming + jnp.einsum(
        "tf,df->td", upper_low, up_weight, preferred_element_type=jnp.float32
    )
    middle_grad = middle_grad.reshape(middle.shape)
    branch_grad = middle_grad.astype(jnp.bfloat16).reshape(windows, groups_here, DILATION, width)
    conv_parts, source_grad = branch_backward(
        source, base_row, groups_here, branch_grad, saved, conv_weight, norm1_gain
    )
    flat_grad = source_grad.reshape(windows, (2 * depth + 1) * rows_here, width)
    gathered = flat_grad[:, depth * rows_here : (depth + 1) * rows_here]
    for slot, offset in enumerate(range(depth, -depth - 1, -1)):
        if offset != 0:
            piece = flat_grad[:, slot * rows_here : (slot + 1) * rows_here]
            gathered = gathered + passed_along(piece, "seq", -offset)
    returned = gathered.astype(jnp.bfloat16)
    input_grad = (keep_mask * (middle_grad + returned.astype(jnp.float32))).astype(jnp.bfloat16)
    conv_grad, conv_bias_grad, gain_one_grad, shift_one_grad = conv_parts
    (
        conv_grad,
        conv_bias_grad,
        gain_one_grad,
        shift_one_grad,
        up_grad,
        up_bias_grad,
        down_grad,
        down_bias_grad,
        gain_two_grad,
        shift_two_grad,
    ) = lax.psum(
        (
            conv_grad,
            conv_bias_grad,
            gain_one_grad,
            shift_one_grad,
            up_grad,
            up_bias_grad,
            down_grad,
            down_bias_grad,
            gain_two_grad,
            shift_two_grad,
        ),
        ("seq", "batch"),
    )
    return (
        block_output,
        input_grad,
        conv_grad,
        conv_bias_grad,
        gain_one_grad,
        shift_one_grad,
        up_grad,
        up_bias_grad,
        down_grad,
        down_bias_grad,
        gain_two_grad,
        shift_two_grad,
    )


def solution(mesh):
    placed = (
        P("batch", "seq", None),
        P("batch"),
        P(),
        P(),
        P(),
        P(),
        P(),
        P(),
        P(),
        P(),
        P(),
        P(),
        P("batch", "seq", None),
    )
    return jax.shard_map(
        per_device,
        mesh=mesh,
        in_specs=placed,
        out_specs=(
            P("batch", "seq", None),
            P("batch", "seq", None),
            P(),
            P(),
            P(),
            P(),
            P(),
            P(),
            P(),
            P(),
            P(),
            P(),
        ),
        check_vma=False,
    )
```

profile of v0, /device:TPU:0, one launch (start us, length us, event | category | flops | bytes accessed | tf_op | source)
XLA Modules:
  0.0 886.9 jit_solution(3291947947895809360)
XLA Ops:
  24.7 9.7 %pad_maximum_fusion = bf16[32,384,512]{2,1,0:T(8,128)(2,1)S(1)} fusion(bf16[32,128,512]{2,1,0:T(8,128)(2,1)S(1)} %collective-permute-done.1, bf16[32,128,512]{2,1,0:T(8,128)(2,1)S(1)} %fusion.40, bf16[32,128,512]{2,1,0:T(8,128)(2,1)S(1)} %collective-permute-done), kind=kLoop, calls=%fused_computation.27 | loop fusion | flops 37748736 | bytes 25165824 | tf_op jit(solution)/shard_map/concatenate | solution.py:124
  34.5 6.3 fusion.121
  52.1 5.8 fusion.130
  63.5 5.7 fusion.136
  69.3 6.1 fusion.139
  81.0 12.2 %fusion.176 = (bf16[32,4,32,512]{3,2,1,0:T(8,128)(2,1)}, bf16[32,4,32,512]{3,2,1,0:T(8,128)(2,1)}, bf16[32,4,32,512]{3,2,1,0:T(8,128)(2,1)}, bf16[32,4,32,512]{3...) fusion(bf16[32,12,32,512]{3,2,1,0:T(8,128)(2,1)S(1)} %bitcast.222), kind=kLoop, calls=%fused_computation.206 | loop fusion | bytes 75497472 | tf_op jit(solution)/shard_map/slice | solution.py:47
  93.3 27.9 %convert_reduce_fusion.2 = (u32[4,32,512]{2,1,0:T(8,128)S(1)}, u32[4,32,512]{2,1,0:T(8,128)S(1)}, f32[32,4,32,512]{3,2,1,0:T(8,128)}) fusion(bf16[32,12,32,512]{3,2,1,0:T(8,128)(2,1)} %bitcast.223, bf16[9,512,512]{2,1,0:T(8,128)(2,1)} %param.33, f32[32,4,32,512]{3,2,1,0:T(8,128)} %fusion.121, f32[32,4,32,512]{3,2,1,0:T(8,128)} %fusion.124, ...), kind=kOutput, calls=%fused_computation.42 | convolution fusion | flops 2189295616 | bytes 89131008 | tf_op jit(solution)/shard_map/wtpd,de->wtpe/dot_general | solution.py:45
  121.1 21.7 %fusion.173 = (f32[32,4,32]{2,1,0:T(4,128)S(1)}, f32[32,4,32,512]{3,2,1,0:T(8,128)S(1)}) fusion(u32[4,32,512]{2,1,0:T(8,128)S(1)} %get-tuple-element.125, f32[32,4,32,512]{3,2,1,0:T(8,128)} %get-tuple-element.163, u32[4,32,512]{2,1,0:T(8,128)S(1)} %get-tuple-element.124), kind=kLoop, calls=%fused_computation.204 | loop fusion | flops 142602240 | bytes 17317888 | tf_op jit(solution)/shard_map/reduce_sum | solution.py:19
  149.3 6.5 fusion.60
  157.8 81.6 %fusion.2 = (bf16[4096,2048]{1,0:T(8,128)(2,1)}, f32[4096,2048]{1,0:T(8,128)}) fusion(f32[2048]{0:T(1024)S(1)} %copy-done.40, bf16[4096,512]{1,0:T(8,128)(2,1)S(1)} %bitcast.233, bf16[512,2048]{1,0:T(8,128)(2,1)S(1)} %copy-done), kind=kOutput, calls=%fused_computation.4 | convolution fusion | flops 9143582720 | bytes 56631296 | tf_op jit(solution)/shard_map/dot_general | solution.py:133
  239.4 12.0 %add_reduce_fusion = (f32[4096]{0:T(1024)S(1)}, f32[4096,512]{1,0:T(8,128)S(1)}) fusion(f32[512]{0:T(512)S(1)} %copy-done.26, bf16[4096,2048]{1,0:T(8,128)(2,1)} %get-tuple-element.164, bf16[2048,512]{1,0:T(8,128)(2,1)S(1)} %copy-done.38), kind=kOutput, calls=%fused_computation.100 | convolution fusion | flops 8594124800 | bytes 27281408 | tf_op jit(solution)/shard_map/dot_general | solution.py:135
  257.6 7.7 convert_reduce_fusion.3
  265.3 13.9 %fusion.178 = f32[2048,512]{1,0:T(8,128)} fusion(bf16[4096,2048]{1,0:T(8,128)(2,1)} %get-tuple-element.164, bf16[4096,512]{1,0:T(8,128)(2,1)S(1)} %get-tuple-element.141), kind=kOutput, calls=%fused_computation.208 | convolution fusion | flops 8589934592 | bytes 25165824 | tf_op jit(solution)/shard_map/tf,td->fd/dot_general | solution.py:143
  279.2 23.1 %convert_reduce_fusion = (f32[2048]{0:T(1024)}, bf16[4096,2048]{1,0:T(8,128)(2,1)}) fusion(f32[4096,2048]{1,0:T(8,128)} %get-tuple-element.165, f32[2048]{0:T(1024)S(1)} %copy-done.40, bf16[4096,512]{1,0:T(8,128)(2,1)S(1)} %get-tuple-element.141, bf16[2048,512]{1,0:T(8,128)(2,1)S(1)} %copy-done.39), kind=kOutput, calls=%fused_computation.11 | convolution fusion | flops 8698984448 | bytes 56639488 | tf_op jit(solution)/shard_map/td,fd->tf/dot_general | solution.py:144
  302.4 16.9 %convert_reduce_fusion.5 = (f32[512]{0:T(512)S(1)}, f32[4096]{0:T(1024)S(1)}, bf16[4096,512]{1,0:T(8,128)(2,1)S(1)}, f32[4096,512]{1,0:T(8,128)}) fusion(f32[512]{0:T(512)S(1)} %copy-done.30, bf16[4096,2048]{1,0:T(8,128)(2,1)} %get-tuple-element.170, bf16[512,2048]{1,0:T(8,128)(2,1)S(1)} %copy-done, f32[32,128,512]{2,1,0:T(8,128)} %get-tuple-element.159), kind=kOutput, calls=%fused_computation.119 | convolution fusion | flops 8602513408 | bytes 39866368 | tf_op jit(solution)/shard_map/tf,df->td/dot_general | solution.py:150
  319.3 16.6 %fusion.177 = f32[512,2048]{1,0:T(8,128)} fusion(bf16[4096,512]{1,0:T(8,128)(2,1)} %bitcast.234, bf16[4096,2048]{1,0:T(8,128)(2,1)} %get-tuple-element.170), kind=kOutput, calls=%fused_computation.207 | convolution fusion | flops 8589934592 | bytes 25165824 | tf_op jit(solution)/shard_map/td,tf->df/dot_general | solution.py:149
  341.4 8.8 convert_reduce_fusion.4
  356.2 9.5 %scatter-add.30 = f32[32,12,32,512]{3,2,1,0:T(8,128)} pad(f32[32,4,32,512]{3,2,1,0:T(8,128)S(1)} %fusion.141, f32[]{:T(128)} %constant.337.clone.1), padding=0_0x0_8x0_0x0_0 | pad | bytes 33554436 | tf_op jit(solution)/shard_map/scatter-add | solution.py:67
  365.7 9.3 %add_dynamic-update-slice_fusion = f32[32,12,32,512]{3,2,1,0:T(8,128)} fusion(f32[32,12,32,512]{3,2,1,0:T(8,128)} %scatter-add.30, bf16[32,4,32,512]{3,2,1,0:T(8,128)(2,1)S(1)} %get-tuple-element.143, bf16[9,512,512]{2,1,0:T(8,128)(2,1)S(1)} %bitcast.231), kind=kOutput, calls=%fused_computation.69 | convolution fusion | flops 2149580800 | bytes 21495808 | tf_op jit(solution)/shard_map/wtpe,de->wtpd/dot_general | solution.py:68
  375.0 9.3 %fusion.32 = f32[32,12,32,512]{3,2,1,0:T(8,128)} fusion(f32[32,12,32,512]{3,2,1,0:T(8,128)} %add_dynamic-update-slice_fusion, bf16[32,4,32,512]{3,2,1,0:T(8,128)(2,1)S(1)} %get-tuple-element.143, bf16[9,512,512]{2,1,0:T(8,128)(2,1)S(1)} %bitcast.231), kind=kOutput, calls=%fused_computation.59 | convolution fusion | flops 2149580800 | bytes 21495808 | tf_op jit(solution)/shard_map/wtpe,de->wtpd/dot_general | solution.py:68
  384.4 9.3 %fusion.31 = f32[32,12,32,512]{3,2,1,0:T(8,128)} fusion(f32[32,12,32,512]{3,2,1,0:T(8,128)} %fusion.32, bf16[32,4,32,512]{3,2,1,0:T(8,128)(2,1)S(1)} %get-tuple-element.143, bf16[9,512,512]{2,1,0:T(8,128)(2,1)S(1)} %bitcast.231), kind=kOutput, calls=%fused_computation.57 | convolution fusion | flops 2149580800 | bytes 21495808 | tf_op jit(solution)/shard_map/wtpe,de->wtpd/dot_general | solution.py:68
  393.6 9.3 %fusion.30 = f32[32,12,32,512]{3,2,1,0:T(8,128)} fusion(f32[32,12,32,512]{3,2,1,0:T(8,128)} %fusion.31, bf16[32,4,32,512]{3,2,1,0:T(8,128)(2,1)S(1)} %get-tuple-element.143, bf16[9,512,512]{2,1,0:T(8,128)(2,1)S(1)} %bitcast.231), kind=kOutput, calls=%fused_computation.55 | convolution fusion | flops 2149580800 | bytes 21495808 | tf_op jit(solution)/shard_map/wtpe,de->wtpd/dot_general | solution.py:68
  402.9 9.2 %fusion.29 = f32[32,12,32,512]{3,2,1,0:T(8,128)} fusion(f32[32,12,32,512]{3,2,1,0:T(8,128)} %fusion.30, bf16[32,4,32,512]{3,2,1,0:T(8,128)(2,1)S(1)} %get-tuple-element.143, bf16[9,512,512]{2,1,0:T(8,128)(2,1)S(1)} %bitcast.231), kind=kOutput, calls=%fused_computation.53 | convolution fusion | flops 2149580800 | bytes 21495808 | tf_op jit(solution)/shard_map/wtpe,de->wtpd/dot_general | solution.py:68
  412.1 9.5 %fusion.28 = f32[32,12,32,512]{3,2,1,0:T(8,128)} fusion(f32[32,12,32,512]{3,2,1,0:T(8,128)} %fusion.29, bf16[32,4,32,512]{3,2,1,0:T(8,128)(2,1)S(1)} %get-tuple-element.143, bf16[9,512,512]{2,1,0:T(8,128)(2,1)S(1)} %bitcast.231), kind=kOutput, calls=%fused_computation.51 | convolution fusion | flops 2149580800 | bytes 21495808 | tf_op jit(solution)/shard_map/wtpe,de->wtpd/dot_general | solution.py:68
  421.6 9.4 %fusion.27 = f32[32,12,32,512]{3,2,1,0:T(8,128)} fusion(f32[32,12,32,512]{3,2,1,0:T(8,128)} %fusion.28, bf16[32,4,32,512]{3,2,1,0:T(8,128)(2,1)S(1)} %get-tuple-element.143, bf16[9,512,512]{2,1,0:T(8,128)(2,1)S(1)} %bitcast.231), kind=kOutput, calls=%fused_computation.49 | convolution fusion | flops 2149580800 | bytes 21495808 | tf_op jit(solution)/shard_map/wtpe,de->wtpd/dot_general | solution.py:68
  431.0 9.4 %fusion.26 = f32[32,12,32,512]{3,2,1,0:T(8,128)} fusion(f32[32,12,32,512]{3,2,1,0:T(8,128)} %fusion.27, bf16[32,4,32,512]{3,2,1,0:T(8,128)(2,1)S(1)} %get-tuple-element.143, bf16[9,512,512]{2,1,0:T(8,128)(2,1)S(1)} %bitcast.231), kind=kOutput, calls=%fused_computation.47 | convolution fusion | flops 2149580800 | bytes 21495808 | tf_op jit(solution)/shard_map/wtpe,de->wtpd/dot_general | solution.py:68
  440.4 11.5 %fusion.175 = (f32[32,128,512]{2,1,0:T(8,128)}, f32[32,128,512]{2,1,0:T(8,128)}) fusion(f32[32,384,512]{2,1,0:T(8,128)} %bitcast.53), kind=kLoop, calls=%fused_computation.205 | loop fusion | bytes 33554432 | tf_op jit(solution)/shard_map/slice | solution.py:162
  453.4 47.3 %collective-permute-start.3 = (f32[32,128,512]{2,1,0:T(8,128)}, f32[32,128,512]{2,1,0:T(8,128)}, u32[]{:S(2)}, u32[]{:S(2)}) collective-permute-start(f32[32,128,512]{2,1,0:T(8,128)} %get-tuple-element.148), channel_id=1, source_target_pairs={{0,4},{4,8},{8,12},{12,16},{16,20},{20,24},{24,28},{1,5},{5,9},{9,... | collective-permute-start | bytes 25165832 | tf_op jit(solution)/shard_map/ppermute | solution.py:15
  528.2 181.6 %all-reduce.1 = (f32[512]{0:T(512)}, f32[512]{0:T(512)}, f32[512]{0:T(512)}, f32[2048]{0:T(1024)}, f32[512]{0:T(512)}, /*index=5*/f32[512]{0:T(512)}, f32[512]{0:T(512)}) all-reduce(f32[512]{0:T(512)S(1)} %get-tuple-element.142, f32[512]{0:T(512)S(1)} %get-tuple-element.122, ...), channel_id=1, replica_groups=mesh['seq'=8,'batch'=4] {'seq','batch'}, use_global_device_ids=true, to_apply=%region_10.0 | all-reduce | flops 5120 | bytes 40960 | tf_op jit(solution)/shard_map/psum | solution.py:178
  709.9 20.7 %multiply_convert_fusion = (bf16[32,128,512]{2,1,0:T(8,128)(2,1)}, bf16[32,128,512]{2,1,0:T(8,128)(2,1)}) fusion(f32[32,128,512]{2,1,0:T(8,128)} %bitcast.232, f32[32,128,512]{2,1,0:T(8,128)} %collective-permute-done.3, f32[32,128,512]{2,1,0:T(8,128)} %collective-permute-done.2, f32[32,384,512]{2,1,0:T(8,128)} %bitcast.53, f32[32,128]{1,0:T(8,128)S(1)} %copy-done.24, ...), kind=kLoop, calls=%fused_computation.68 | loop fusion | flops 29360128 | bytes 58736640 | tf_op jit(solution)/shard_map/convert_element_type | solution.py:165
  730.5 134.6 %all-reduce.5.cloned.1.call-done = (f32[9,512,512]{2,1,0:T(8,128)}, f32[512,2048]{1,0:T(8,128)}, f32[2048,512]{1,0:T(8,128)}) async-done(((f32[9,512,512]{2,1,0:T(8,128)}, f32[512,2048]{1,0:T(8,128)}, f32[2048,512]{1,0:T(8,128)}), (f32[9,512,512]{2,1,0:T(8,128)}, f32[512,2048]{1,0:T(8,128)}, f32[2048,512]{1,0:T(8,128)})) %all-reduce.5.cloned.1.call-update) | async-done | bytes 17825808 | tf_op jit(solution)/shard_map/psum | solution.py:178
  865.2 8.7 copy.188
  (139 shorter events, 100.6 us)
Async XLA Ops:
  7.2 150.6 %copy-start = (bf16[512,2048]{1,0:T(8,128)(2,1)S(1)}, bf16[512,2048]{1,0:T(8,128)(2,1)}, u32[]{:S(2)}) copy-start(bf16[512,2048]{1,0:T(8,128)(2,1)} %param.37) | copy-start | bytes 6291460
  7.2 858.0 %all-reduce.5.cloned.1.call-start = ((), (), s32[]{:S(2)}) async-start(), calls=%async_computation | async-start | bytes 35651584 | tf_op jit(solution)/shard_map/psum | solution.py:178
  8.1 140.6 %copy-start.23 = (f32[32,128]{1,0:T(8,128)}, f32[32,128]{1,0:T(8,128)S(1)}, u32[]{:S(2)}) copy-start(f32[32,128]{1,0:T(8,128)S(1)} %compare_convert_fusion) | copy-start | bytes 49156
  8.1 26.3 %slice-start.2 = ((s8[4718592]{0:T(1024)(128)(4,1)}), s8[4194304]{0:T(1024)(128)(4,1)S(1)}, s32[]{:S(2)}) async-start(s8[4718592]{0:T(1024)(128)(4,1)} %bitcast.228), calls=%async_computation.3 | async-start | bytes 8388608
  11.0 23.5 %slice-start.3 = ((s8[4718592]{0:T(1024)(128)(4,1)}), s8[524288]{0:T(1024)(128)(4,1)S(1)}, s32[]{:S(2)}) async-start(s8[4718592]{0:T(1024)(128)(4,1)} %bitcast.228), calls=%async_computation.4 | async-start | bytes 1048576
  11.0 9.3 %collective-permute-start = (bf16[32,128,512]{2,1,0:T(8,128)(2,1)S(1)}, bf16[32,128,512]{2,1,0:T(8,128)(2,1)S(1)}, u32[]{:S(2)}, u32[]{:S(2)}) collective-permute-start(bf16[32,128,512]{2,1,0:T(8,128)(2,1)S(1)} %fusion.40), channel_id=1, source_target_pairs={{0,4},{4,8},{8,12},{12,16},{16,20},{20,24},{24,28},{1,5},{5,9},{9,... | collective-permute-start | bytes 12582920 | tf_op jit(solution)/shard_map/ppermute | solution.py:15
  13.8 11.0 %collective-permute-start.1 = (bf16[32,128,512]{2,1,0:T(8,128)(2,1)S(1)}, bf16[32,128,512]{2,1,0:T(8,128)(2,1)S(1)}, u32[]{:S(2)}, u32[]{:S(2)}) collective-permute-start(bf16[32,128,512]{2,1,0:T(8,128)(2,1)S(1)} %fusion.40), channel_id=1, source_target_pairs={{4,0},{8,4},{12,8},{16,12},{20,16},{24,20},{28,24},{5,1},{9,5},{13... | collective-permute-start | bytes 12582920 | tf_op jit(solution)/shard_map/ppermute | solution.py:15
  34.4 46.6 %copy-start.1 = (bf16[32,384,512]{2,1,0:T(8,128)(2,1)}, bf16[32,384,512]{2,1,0:T(8,128)(2,1)S(1)}, u32[]{:S(2)}) copy-start(bf16[32,384,512]{2,1,0:T(8,128)(2,1)S(1)} %pad_maximum_fusion) | copy-start | bytes 37748740
  81.0 12.2 %copy-start.35 = (f32[512]{0:T(512)S(1)}, f32[512]{0:T(512)}, u32[]{:S(2)}) copy-start(f32[512]{0:T(512)} %param.34) | copy-start | bytes 6148
  144.3 4.4 copy-start.4
  144.3 4.9 copy-start.17
  144.3 4.9 copy-start.27
  149.3 6.5 copy-start.5
  149.3 8.5 copy-start.40
  157.8 81.6 %copy-start.26 = (f32[512]{0:T(512)S(1)}, f32[512]{0:T(512)}, u32[]{:S(2)}) copy-start(f32[512]{0:T(512)} %param.40) | copy-start | bytes 6148
  157.8 81.6 %copy-start.38 = (bf16[2048,512]{1,0:T(8,128)(2,1)S(1)}, bf16[2048,512]{1,0:T(8,128)(2,1)}, u32[]{:S(2)}) copy-start(bf16[2048,512]{1,0:T(8,128)(2,1)} %param.39) | copy-start | bytes 6291460
  239.4 13.8 %slice-start = ((s8[8388608]{0:T(1024)(128)(4,1)}), s8[4194304]{0:T(1024)(128)(4,1)S(1)}, s32[]{:S(2)}) async-start(s8[8388608]{0:T(1024)(128)(4,1)} %bitcast.224), calls=%async_computation.1 | async-start | bytes 8388608
  239.4 13.8 %slice-start.1 = ((s8[8388608]{0:T(1024)(128)(4,1)}), s8[4194304]{0:T(1024)(128)(4,1)S(1)}, s32[]{:S(2)}) async-start(s8[8388608]{0:T(1024)(128)(4,1)} %bitcast.224), calls=%async_computation.2 | async-start | bytes 8388608
  253.2 4.3 copy-start.25
  265.3 13.9 %copy-start.39 = (bf16[2048,512]{1,0:T(8,128)(2,1)S(1)}, bf16[2048,512]{1,0:T(8,128)(2,1)}, u32[]{:S(2)}) copy-start(bf16[2048,512]{1,0:T(8,128)(2,1)} %param.39) | copy-start | bytes 6291460
  279.2 23.1 %copy-start.30 = (f32[512]{0:T(512)S(1)}, f32[512]{0:T(512)}, u32[]{:S(2)}) copy-start(f32[512]{0:T(512)} %param.35) | copy-start | bytes 6148
  319.3 16.6 %copy-start.3 = (bf16[4096,512]{1,0:T(8,128)(2,1)}, bf16[4096,512]{1,0:T(8,128)(2,1)S(1)}, u32[]{:S(2)}) copy-start(bf16[4096,512]{1,0:T(8,128)(2,1)S(1)} %get-tuple-element.144) | copy-start | bytes 12582916
  319.3 16.6 %copy-start.20 = (f32[32,4,32]{2,1,0:T(4,128)S(1)}, f32[32,4,32]{2,1,0:T(4,128)}, u32[]{:S(2)}) copy-start(f32[32,4,32]{2,1,0:T(4,128)} %copy-done.19) | copy-start | bytes 49156
  319.3 16.6 %copy-start.22 = (f32[32,4,32]{2,1,0:T(4,128)S(1)}, f32[32,4,32]{2,1,0:T(4,128)}, u32[]{:S(2)}) copy-start(f32[32,4,32]{2,1,0:T(4,128)} %copy-done.21) | copy-start | bytes 49156
  335.9 14.3 %slice-start.4 = ((s8[4718592]{0:T(1024)(128)(4,1)}), s8[524288]{0:T(1024)(128)(4,1)S(1)}, s32[]{:S(2)}) async-start(s8[4718592]{0:T(1024)(128)(4,1)} %bitcast.230), calls=%async_computation.5 | async-start | bytes 1048576
  341.4 8.8 slice-start.5
  440.4 60.4 %copy-start.13 = (bf16[32,4,32,512]{3,2,1,0:T(8,128)(2,1)S(1)}, bf16[32,4,32,512]{3,2,1,0:T(8,128)(2,1)}, u32[]{:S(2)}) copy-start(bf16[32,4,32,512]{3,2,1,0:T(8,128)(2,1)} %get-tuple-element.156) | copy-start | bytes 12582916
  451.8 52.2 %copy-start.12 = (bf16[32,4,32,512]{3,2,1,0:T(8,128)(2,1)S(1)}, bf16[32,4,32,512]{3,2,1,0:T(8,128)(2,1)}, u32[]{:S(2)}) copy-start(bf16[32,4,32,512]{3,2,1,0:T(8,128)(2,1)} %get-tuple-element.155) | copy-start | bytes 12582916
  451.9 258.0 %collective-permute-start.2 = (f32[32,128,512]{2,1,0:T(8,128)}, f32[32,128,512]{2,1,0:T(8,128)}, u32[]{:S(2)}, u32[]{:S(2)}) collective-permute-start(f32[32,128,512]{2,1,0:T(8,128)} %get-tuple-element.147), channel_id=1, source_target_pairs={{4,0},{8,4},{12,8},{16,12},{20,16},{24,20},{28,24},{5,1},{9,5},{13... | collective-permute-start | bytes 25165832 | tf_op jit(solution)/shard_map/ppermute | solution.py:15
  453.4 256.5 %collective-permute-start.3 = (f32[32,128,512]{2,1,0:T(8,128)}, f32[32,128,512]{2,1,0:T(8,128)}, u32[]{:S(2)}, u32[]{:S(2)}) collective-permute-start(f32[32,128,512]{2,1,0:T(8,128)} %get-tuple-element.148), channel_id=1, source_target_pairs={{0,4},{4,8},{8,12},{12,16},{16,20},{20,24},{24,28},{1,5},{5,9},{9,... | collective-permute-start | bytes 25165832 | tf_op jit(solution)/shard_map/ppermute | solution.py:15
  527.5 182.3 %copy-start.24 = (f32[32,128]{1,0:T(8,128)S(1)}, f32[32,128]{1,0:T(8,128)}, u32[]{:S(2)}) copy-start(f32[32,128]{1,0:T(8,128)} %copy-done.23) | copy-start | bytes 49156
  865.2 8.7 copy-start.16
  (20 other events, 53.3 us)
Sparse Core Ops, SparseCore 0:
  527.7 337.4 all-reduce.4
where the time goes:
time: 891 us; the launch traced here: 887 us
  matrix products  346 us (39%)
  blocking collectives  182 us (20%)
  waiting for transfers between devices  144 us (16%)
  other arithmetic  93.4 us (10%)
  local copies, waits for them, and re-layouts  53.8 us (6%)
  starting transfers between devices  53 us (6%)
  between operations  15.1 us (2%)
    psum x1, blocking collectives, per_device(): lax.psum((conv_grad, conv_bias_grad, gain_one_grad, shift_one_grad, up_gr...  182 us
    psum x1, waiting for transfers between devices, per_device(): lax.psum((conv_grad, conv_bias_grad, gain_one_grad, shift_one_grad, up_gr...  135 us
    dot_general x1, matrix products, per_device(): jnp.dot(middle_low, up_weight, preferred_element_type=jnp.float32) + up_bias  81.6 us
    dot_general x9, matrix products, taps_grads(): jnp.einsum('wtpe,de->wtpd', grad_low, weight[tap_index], preferred_elemen...  77.2 us
    dot_general x9, matrix products, taps_apply(): jnp.einsum('wtpd,de->wtpe', source[:, begin:begin + count], weight[tap_in...  74.4 us
    ppermute x4, starting transfers between devices, passed_along(): return lax.ppermute(shard, axis, pairs)  52.9 us
    dot_general x9, matrix products, taps_grads(): jnp.einsum('wtpd,wtpe->de', source[:, begin:begin + count], grad_low, pre...  30 us
    dot_general x1, matrix products, per_device(): jnp.einsum('td,fd->tf', lower_low, down_weight, preferred_element_type=jn...  23.1 us
  transfers between devices with their start and end apart: 5, of which 3 were waited for; matrix products, arithmetic and copies ran while one was open for 5% of the time, Pallas kernels for 0%

commit v1 on v0

v1 whole, which is shorter than its diff:
```python
import functools
import math

import jax
import jax.numpy as jnp
from jax import lax
from jax.experimental import pallas as pl
from jax.experimental.pallas import tpu as pltpu
from jax.sharding import PartitionSpec as P

KERNEL = 9
DILATION = 32
REACH = DILATION * (KERNEL // 2)
TILE_ROWS = 512
FF_TILE = 512
EPS = 1e-05
VMEM_BYTES = 62 * 2**20


def passed_along(shard, axis, by):
    size = lax.axis_size(axis)
    pairs = [(i, i + by) for i in range(size) if 0 <= i + by < size]
    return lax.ppermute(shard, axis, pairs)


def dot(left, right):
    return jnp.dot(left, right, preferred_element_type=jnp.float32)


def gelu_parts(values):
    cumulative = 0.5 + 0.5 * lax.erf(values * (1.0 / math.sqrt(2.0)))
    density = jnp.exp(-0.5 * values * values) * (1.0 / math.sqrt(2.0 * math.pi))
    return values * cumulative, cumulative + values * density


def normalize(values):
    center = jnp.mean(values, axis=-1, keepdims=True)
    centered = values - center
    inverse = lax.rsqrt(jnp.mean(centered * centered, axis=-1, keepdims=True) + EPS)
    return centered * inverse, inverse


def normalize_back(upstream, normed, inverse, gain):
    inner = upstream * gain
    return inverse * (
        inner
        - jnp.mean(inner, axis=-1, keepdims=True)
        - normed * jnp.mean(inner * normed, axis=-1, keepdims=True)
    )


def col_sum(values):
    return jnp.sum(values, axis=0, keepdims=True)


def block_kernel(depth, *refs):
    pieces = 2 * depth + 1
    keeps = refs[0]
    parts = refs[1 : 1 + pieces]
    (
        cot,
        conv_w,
        conv_b,
        gain1,
        bias1,
        up_w,
        up_wt,
        up_b,
        down_w,
        down_wt,
        down_b,
        gain2,
        bias2,
        out,
        pre_out,
        mid_out,
        d_up,
        d_down,
        d_vec,
        d_upb,
        ext,
        hidden,
        slope,
    ) = refs[1 + pieces :]
    step = pl.program_id(0)
    group, rows_here, width = cot.shape
    rows = group * rows_here
    ff = up_w.shape[1]
    tile = min(FF_TILE, ff)
    base = depth * rows_here - REACH

    @pl.when(step == 0)
    def _():
        d_up[...] = jnp.zeros_like(d_up)
        d_down[...] = jnp.zeros_like(d_down)
        d_vec[...] = jnp.zeros_like(d_vec)
        d_upb[...] = jnp.zeros_like(d_upb)

    keep_here = []
    for g in range(group):
        window = step * group + g
        for i in range(pieces):
            keep = keeps[i, window]
            if i == depth:
                keep_here.append(keep)
            ext[g, i * rows_here : (i + 1) * rows_here, :] = parts[i][g] * keep.astype(jnp.bfloat16)

    pre = jnp.broadcast_to(conv_b[...], (rows, width))
    for tap in range(KERNEL):
        begin = base + tap * DILATION
        taken = ext[:, begin : begin + rows_here, :].reshape(rows, width)
        pre = pre + dot(taken, conv_w[tap])
    act, slope1 = gelu_parts(pre)
    n1, s1 = normalize(act)
    branch = (n1 * gain1[...] + bias1[...]).astype(jnp.bfloat16)
    start = ext[:, depth * rows_here : (depth + 1) * rows_here, :].reshape(rows, width)
    middle = start.astype(jnp.float32) + branch.astype(jnp.float32)
    middle_low = middle.astype(jnp.bfloat16)

    lower = jnp.broadcast_to(down_b[...], (rows, width))
    for j in range(ff // tile):
        cols = slice(j * tile, (j + 1) * tile)
        upper = dot(middle_low, up_w[:, cols]) + up_b[:, cols]
        h, sl = gelu_parts(upper)
        h = h.astype(jnp.bfloat16)
        hidden[:, cols] = h
        slope[:, cols] = sl
        lower = lower + dot(h, down_w[cols, :])
    n2, s2 = normalize(lower)
    shaped = (n2 * gain2[...] + bias2[...] + middle).reshape(group, rows_here, width)
    incoming = []
    for g in range(group):
        out[g] = (shaped[g] * keep_here[g]).astype(jnp.bfloat16)
        incoming.append(cot[g].astype(jnp.float32) * keep_here[g])
    incoming = jnp.concatenate(incoming, axis=0)
    d_vec[0:1, :] += col_sum(incoming * n2)
    d_vec[1:2, :] += col_sum(incoming)
    lower_low = normalize_back(incoming, n2, s2, gain2[...]).astype(jnp.bfloat16)
    d_vec[2:3, :] += col_sum(lower_low.astype(jnp.float32))
    lower_t = lower_low.T
    middle_t = middle_low.T
    middle_grad = incoming
    for j in range(ff // tile):
        cols = slice(j * tile, (j + 1) * tile)
        hidden_grad = dot(lower_low, down_wt[:, cols])
        upper_grad = hidden_grad * slope[:, cols]
        upper_low = upper_grad.astype(jnp.bfloat16)
        d_upb[:, cols] += col_sum(upper_low.astype(jnp.float32))
        d_down[:, cols] += dot(lower_t, hidden[:, cols])
        d_up[:, cols] += dot(middle_t, upper_low)
        middle_grad = middle_grad + dot(upper_low, up_wt[cols, :])
    branch_low = middle_grad.astype(jnp.bfloat16)
    mid_out[...] = branch_low.reshape(group, rows_here, width)
    branch_grad = branch_low.astype(jnp.float32)
    d_vec[3:4, :] += col_sum(branch_grad * n1)
    d_vec[4:5, :] += col_sum(branch_grad)
    pre_low = (normalize_back(branch_grad, n1, s1, gain1[...]) * slope1).astype(jnp.bfloat16)
    d_vec[5:6, :] += col_sum(pre_low.astype(jnp.float32))
    pre_out[...] = pre_low.reshape(group, rows_here, width)


def blocks(keeps, parts, cot, conv_w, conv_b, gain1, bias1, up_w, up_wt, up_b, down_w, down_wt, down_b, gain2, bias2):
    windows, rows_here, width = cot.shape
    depth = len(parts) // 2
    ff = up_w.shape[1]
    group = max(1, TILE_ROWS // rows_here)
    rows = group * rows_here
    tile = pl.BlockSpec((group, rows_here, width), lambda i: (i, 0, 0))
    whole = pl.BlockSpec(memory_space=pltpu.VMEM)
    whole_params = [conv_w, conv_b, gain1, bias1, up_w, up_wt, up_b, down_w, down_wt, down_b, gain2, bias2]
    return pl.pallas_call(
        functools.partial(block_kernel, depth),
        grid=(windows // group,),
        in_specs=[pl.BlockSpec(memory_space=pltpu.SMEM)] + [tile] * (len(parts) + 1) + [whole] * len(whole_params),
        out_specs=[tile, tile, tile, whole, whole, whole, whole],
        out_shape=[jax.ShapeDtypeStruct(cot.shape, jnp.bfloat16)] * 3
        + [
            jax.ShapeDtypeStruct((width, ff), jnp.float32),
            jax.ShapeDtypeStruct((width, ff), jnp.float32),
            jax.ShapeDtypeStruct((8, width), jnp.float32),
            jax.ShapeDtypeStruct((1, ff), jnp.float32),
        ],
        scratch_shapes=[
            pltpu.VMEM((group, (2 * depth + 1) * rows_here, width), jnp.bfloat16),
            pltpu.VMEM((rows, ff), jnp.bfloat16),
            pltpu.VMEM((rows, ff), jnp.float32),
        ],
        compiler_params=pltpu.CompilerParams(vmem_limit_bytes=VMEM_BYTES),
        name="block",
    )(keeps, *parts, cot, *whole_params)


def back_kernel(depth, *refs):
    pieces = 2 * depth + 1
    keeps = refs[0]
    parts = refs[1 : 1 + pieces]
    start_in, mid_in, conv_wt, out, d_conv, ext = refs[1 + pieces :]
    step = pl.program_id(0)
    group, rows_here, width = start_in.shape
    rows = group * rows_here
    base = depth * rows_here - REACH

    @pl.when(step == 0)
    def _():
        d_conv[...] = jnp.zeros_like(d_conv)

    start = []
    for g in range(group):
        start.append(start_in[g] * keeps[depth, step * group + g].astype(jnp.bfloat16))
        for i in range(pieces):
            ext[g, i * rows_here : (i + 1) * rows_here, :] = parts[i][g]
    start_t = jnp.concatenate(start, axis=0).T
    grad = jnp.zeros((rows, width), jnp.float32)
    for tap in range(KERNEL):
        begin = base + (KERNEL - 1 - tap) * DILATION
        taken = ext[:, begin : begin + rows_here, :].reshape(rows, width)
        d_conv[tap] += dot(start_t, taken)
        grad = grad + dot(taken, conv_wt[tap])
    grad = grad.astype(jnp.bfloat16).astype(jnp.float32) + mid_in[...].reshape(rows, width).astype(jnp.float32)
    grad = grad.reshape(group, rows_here, width)
    for g in range(group):
        out[g] = (grad[g] * keeps[depth, step * group + g]).astype(jnp.bfloat16)


def conv_back(keeps, parts, start, mid, conv_wt):
    windows, rows_here, width = start.shape
    depth = len(parts) // 2
    group = max(1, TILE_ROWS // rows_here)
    tile = pl.BlockSpec((group, rows_here, width), lambda i: (i, 0, 0))
    whole = pl.BlockSpec(memory_space=pltpu.VMEM)
    return pl.pallas_call(
        functools.partial(back_kernel, depth),
        grid=(windows // group,),
        in_specs=[pl.BlockSpec(memory_space=pltpu.SMEM)] + [tile] * (len(parts) + 2) + [whole],
        out_specs=[tile, whole],
        out_shape=[
            jax.ShapeDtypeStruct(start.shape, jnp.bfloat16),
            jax.ShapeDtypeStruct((KERNEL, width, width), jnp.float32),
        ],
        scratch_shapes=[pltpu.VMEM((group, (2 * depth + 1) * rows_here, width), jnp.bfloat16)],
        compiler_params=pltpu.CompilerParams(vmem_limit_bytes=VMEM_BYTES),
        name="conv_back",
    )(keeps, *parts, start, mid, conv_wt)


def spread(shard, depth):
    return [
        shard if offset == 0 else passed_along(shard, "seq", offset)
        for offset in range(depth, -depth - 1, -1)
    ]


def per_device(
    block_input,
    window_lengths,
    conv_weight,
    conv_bias,
    norm1_gain,
    norm1_bias,
    up_weight,
    up_bias,
    down_weight,
    down_bias,
    norm2_gain,
    norm2_bias,
    out_cotangent,
):
    windows, rows_here, width = block_input.shape
    depth = -(-REACH // rows_here)
    parts = spread(block_input, depth)
    first = (lax.axis_index("seq") + jnp.arange(-depth, depth + 1, dtype=jnp.int32)) * rows_here
    keeps = (first[:, None] < window_lengths[None, :]).astype(jnp.float32)
    row = lambda v: v.reshape(1, -1)
    conv_wt = conv_weight.transpose(0, 2, 1)
    out, pre_low, mid_low, d_up, d_down_t, d_vec, d_upb = blocks(
        keeps,
        parts,
        out_cotangent,
        conv_weight,
        row(conv_bias),
        row(norm1_gain),
        row(norm1_bias),
        up_weight,
        up_weight.T,
        row(up_bias),
        down_weight,
        down_weight.T,
        row(down_bias),
        row(norm2_gain),
        row(norm2_bias),
    )
    input_grad, d_conv = conv_back(keeps, spread(pre_low, depth), block_input, mid_low, conv_wt)
    d_conv, d_up, d_down_t, d_vec, d_upb = lax.psum((d_conv, d_up, d_down_t, d_vec, d_upb), ("seq", "batch"))
    return (
        out,
        input_grad,
        d_conv,
        d_vec[5],
        d_vec[3],
        d_vec[4],
        d_up,
        d_upb[0],
        d_down_t.T,
        d_vec[2],
        d_vec[0],
        d_vec[1],
    )


def solution(mesh):
    rows = P("batch", "seq", None)
    return jax.shard_map(
        per_device,
        mesh=mesh,
        in_specs=(rows, P("batch")) + (P(),) * 10 + (rows,),
        out_specs=(rows, rows) + (P(),) * 10,
        check_vma=False,
    )
```

time: 891 us -> 580 us (0.65)
  matrix products: 346 us -> 0 us
  Pallas kernels: 0 us -> 149 us
  waiting for transfers between devices: 144 us -> 251 us
  blocking collectives: 182 us -> 83.1 us
  other arithmetic: 93.4 us -> 0.65 us
  local copies, waits for them, and re-layouts: 53.8 us -> 30.3 us
    dot_general x33 -> x0, matrix products: 346 us -> none  [the longest x1 81.6 us: per_device(): jnp.dot(middle_low, up_weight, preferred_element_type=jnp.float32) + up_bias]
    pallas_call x0 -> x2, Pallas kernels: none -> 149 us  [the longest x1 99.7 us: blocks(): pl.pallas_call(functools.partial(block_kernel, depth), grid=(windows // g...]
    psum x1, waiting for transfers between devices: 135 us -> 251 us  [per_device(): lax.psum((d_conv, d_up, d_down_t, d_vec, d_upb), ('seq', 'batch'))]
    psum x1, blocking collectives: 182 us -> 83.1 us  [per_device(): lax.psum((d_conv, d_up, d_down_t, d_vec, d_upb), ('seq', 'batch'))]
    reduce_sum x8 -> x0, other arithmetic: 57.5 us -> none  [the longest x1 21.7 us: normalize(): center = jnp.mean(values, axis=-1, keepdims=True)]
    convert_element_type x4 -> x1, other arithmetic: 26 us -> 0.65 us  [per_device(): keeps = (first[:, None] < window_lengths[None, :]).astype(jnp.float32)]
    slice x2 -> x1, local copies, waits for them, and re-layouts: 23.7 us -> 0.6 us  [per_device(): d_vec[1]]
    concatenate x1 -> x0, other arithmetic: 9.69 us -> none  [per_device(): extended = jnp.concatenate(pieces, axis=1)]
  transfers between devices with their start and end apart: 5 -> 5, of which waited for: 3 -> 1; matrix products, arithmetic and copies ran while one was open for 5% -> 2% of each run, Pallas kernels for 0% -> 0%
where the time goes in v1:
time: 580 us; the launch traced here: 579 us
  waiting for transfers between devices  251 us (43%)
  Pallas kernels  149 us (26%)
  blocking collectives  83.1 us (14%)
  starting transfers between devices  51.8 us (9%)
  local copies, waits for them, and re-layouts  30.3 us (5%)
  between operations  14.1 us (2%)
    psum x1, waiting for transfers between devices, per_device(): lax.psum((d_conv, d_up, d_down_t, d_vec, d_upb), ('seq', 'batch'))  251 us
    pallas_call x1, Pallas kernels, blocks(): pl.pallas_call(functools.partial(block_kernel, depth), grid=(windows // g...  99.7 us
    psum x1, blocking collectives, per_device(): lax.psum((d_conv, d_up, d_down_t, d_vec, d_upb), ('seq', 'batch'))  83.1 us
    ppermute x4, starting transfers between devices, passed_along(): return lax.ppermute(shard, axis, pairs)  51.8 us
    pallas_call x1, Pallas kernels, conv_back(): pl.pallas_call(functools.partial(back_kernel, depth), grid=(windows // gr...  49.2 us
    unnamed x16, local copies, waits for them, and re-layouts  29.7 us
  transfers between devices with their start and end apart: 5, of which 1 were waited for; matrix products, arithmetic and copies ran while one was open for 2% of the time, Pallas kernels for 0%

profile of v1, /device:TPU:0, one launch (start us, length us, event | category | flops | bytes accessed | tf_op | source)
XLA Modules:
  0.0 579.5 jit_solution(10735000858727728382)
XLA Ops:
  7.2 0.0 copy-start
  7.2 0.0 all-reduce.4.cloned.1.call-start
  7.2 1.4 collective-permute-start.1
  8.7 5.0 collective-permute-start
  13.7 0.0 copy-start.4
  13.7 3.9 copy.25
  17.6 0.0 copy-done
  17.6 2.4 copy.26
  20.0 0.0 copy-done.4
  20.0 0.6 compare_convert_fusion.refs_0_
  20.6 0.0 collective-permute-done.1.refs_3_
  20.6 0.0 collective-permute-done.refs_1_
  20.6 99.7 %block.1 = (bf16[32,128,512]{2,1,0:T(8,128)(2,1)}, bf16[32,128,512]{2,1,0:T(8,128)(2,1)}, bf16[32,128,512]{2,1,0:T(8,128)(2,1)}, f32[512,2048]{1,0:T(8,128)}, f3...) custom-call(f32[3,32]{1,0:T(4,128)} %compare_convert_fusion.refs_0_, ...), custom_call_target="tpu_custom_call" | custom-call | tf_op jit(solution)/shard_map/block/pallas_call | solution.py:171
  120.3 1.3 collective-permute-start.3
  121.6 44.0 %collective-permute-start.2 = (bf16[32,128,512]{2,1,0:T(8,128)(2,1)}, bf16[32,128,512]{2,1,0:T(8,128)(2,1)}, u32[]{:S(2)}, u32[]{:S(2)}) collective-permute-start(bf16[32,128,512]{2,1,0:T(8,128)(2,1)} %get-tuple-element.22.refs_2_), channel_id=1, source_target_pairs={{0,4},{4,8},{8,12},{12,16},{16,20},{20,24},{24,28},{1,5},{5,9},{9,... | collective-permute-start | bytes 12582920 | tf_op jit(solution)/shard_map/ppermute | solution.py:23
  165.7 6.6 %copy.27 = bf16[9,512,512]{1,2,0:T(8,128)(2,1)} copy(bf16[9,512,512]{2,1,0:T(8,128)(2,1)} %refs_5_.1) | data formatting | bytes 9437184 | tf_op args[2]
  172.3 0.0 collective-permute-done.3.refs_3_
  172.3 0.0 collective-permute-done.2.refs_1_
  172.3 49.2 %conv_back.1 = (bf16[32,128,512]{2,1,0:T(8,128)(2,1)}, f32[9,512,512]{2,1,0:T(8,128)}) custom-call(f32[3,32]{1,0:T(4,128)} %compare_convert_fusion.refs_0_, bf16[32,128,512]{2,1,0:T(8,128)(2,1)} %collective-permute-done.2.refs_1_, bf16[32,128,512]{2,1,0:T(8,128)(2,1)} %get-tuple-element.22.refs_2_, bf16[32,128,512]{2,1,0:T(8,128)(2,1)} %collective-permute-done.3.refs_3_, ...), custom_call_target="tpu_custom_call" | custom-call | tf_op jit(solution)/shard_map/conv_back/pallas_call | solution.py:231
  221.5 0.0 copy-start.2
  221.5 0.0 copy-start.3
  221.5 0.0 all-reduce.4.cloned.1.call-update
  221.6 0.7 copy-done.2
  222.2 0.0 copy-done.3
  222.2 83.1 %all-reduce = (f32[8,512]{1,0:T(8,128)S(1)}, f32[2048]{0:T(1024)}) all-reduce(f32[8,512]{1,0:T(8,128)S(1)} %copy-done.2, f32[2048]{0:T(1024)S(1)} %bitcast.22), channel_id=1, replica_groups=mesh['seq'=8,'batch'=4] {'seq','batch'}, use_global_device_ids=true, to_apply=%region_1.0 | all-reduce | flops 6144 | bytes 49152 | tf_op jit(solution)/shard_map/psum | solution.py:293
  305.4 0.6 fusion
  306.0 250.6 %all-reduce.4.cloned.1.call-done = (f32[9,512,512]{2,1,0:T(8,128)}, f32[512,2048]{1,0:T(8,128)}, f32[2048,512]{0,1:T(8,128)}) async-done(((f32[9,512,512]{2,1,0:T(8,128)}, f32[512,2048]{1,0:T(8,128)}, f32[2048,512]{0,1:T(8,128)}), (f32[9,512,512]{2,1,0:T(8,128)}, f32[512,2048]{1,0:T(8,128)}, f32[2048,512]{0,1:T(8,128)})) %all-reduce.4.cloned.1.call-update) | async-done | bytes 17825808 | tf_op jit(solution)/shard_map/psum | solution.py:293
  556.6 5.3 copy.28
  561.9 0.0 copy-start.1
  561.9 8.7 %copy.32 = f32[9,512,512]{2,1,0:T(8,128)} copy(f32[9,512,512]{2,1,0:T(8,128)} %get-tuple-element.55) | data formatting | bytes 18874368
  570.6 0.0 copy-done.1
  570.6 2.0 copy.33
  (1 shorter events, 0.0 us)
Async XLA Ops:
  7.2 10.4 %copy-start = (bf16[2048,512]{1,0:T(8,128)(2,1)S(1)}, bf16[2048,512]{1,0:T(8,128)(2,1)}, u32[]{:S(2)}) copy-start(bf16[2048,512]{1,0:T(8,128)(2,1)} %refs_12_.1) | copy-start | bytes 6291460
  7.2 549.4 %all-reduce.4.cloned.1.call-start = ((), (), s32[]{:S(2)}) async-start(), calls=%async_computation | async-start | bytes 35651584 | tf_op jit(solution)/shard_map/psum | solution.py:293
  7.2 13.4 %collective-permute-start.1 = (bf16[32,128,512]{2,1,0:T(8,128)(2,1)}, bf16[32,128,512]{2,1,0:T(8,128)(2,1)}, u32[]{:S(2)}, u32[]{:S(2)}) collective-permute-start(bf16[32,128,512]{2,1,0:T(8,128)(2,1)} %refs_4_.3), channel_id=1, source_target_pairs={{4,0},{8,4},{12,8},{16,12},{20,16},{24,20},{28,24},{5,1},{9,5},{13... | collective-permute-start | bytes 12582920 | tf_op jit(solution)/shard_map/ppermute | solution.py:23
  8.7 12.0 %collective-permute-start = (bf16[32,128,512]{2,1,0:T(8,128)(2,1)}, bf16[32,128,512]{2,1,0:T(8,128)(2,1)}, u32[]{:S(2)}, u32[]{:S(2)}) collective-permute-start(bf16[32,128,512]{2,1,0:T(8,128)(2,1)} %refs_4_.3), channel_id=1, source_target_pairs={{0,4},{4,8},{8,12},{12,16},{16,20},{20,24},{24,28},{1,5},{5,9},{9,... | collective-permute-start | bytes 12582920 | tf_op jit(solution)/shard_map/ppermute | solution.py:23
  13.7 6.3 %copy-start.4 = (s32[32]{0:T(128)S(1)}, s32[32]{0:T(128)}, u32[]{:S(2)}) copy-start(s32[32]{0:T(128)} %param.14) | copy-start | bytes 388
  120.3 52.0 %collective-permute-start.3 = (bf16[32,128,512]{2,1,0:T(8,128)(2,1)}, bf16[32,128,512]{2,1,0:T(8,128)(2,1)}, u32[]{:S(2)}, u32[]{:S(2)}) collective-permute-start(bf16[32,128,512]{2,1,0:T(8,128)(2,1)} %get-tuple-element.22.refs_2_), channel_id=1, source_target_pairs={{4,0},{8,4},{12,8},{16,12},{20,16},{24,20},{28,24},{5,1},{9,5},{13... | collective-permute-start | bytes 12582920 | tf_op jit(solution)/shard_map/ppermute | solution.py:23
  121.6 50.7 %collective-permute-start.2 = (bf16[32,128,512]{2,1,0:T(8,128)(2,1)}, bf16[32,128,512]{2,1,0:T(8,128)(2,1)}, u32[]{:S(2)}, u32[]{:S(2)}) collective-permute-start(bf16[32,128,512]{2,1,0:T(8,128)(2,1)} %get-tuple-element.22.refs_2_), channel_id=1, source_target_pairs={{0,4},{4,8},{8,12},{12,16},{16,20},{20,24},{24,28},{1,5},{5,9},{9,... | collective-permute-start | bytes 12582920 | tf_op jit(solution)/shard_map/ppermute | solution.py:23
  221.5 0.7 copy-start.2
  221.5 0.7 copy-start.3
  561.9 8.7 %copy-start.1 = (f32[512,2048]{1,0:T(8,128)S(1)}, f32[512,2048]{1,0:T(8,128)}, u32[]{:S(2)}) copy-start(f32[512,2048]{1,0:T(8,128)} %get-tuple-element.59) | copy-start | bytes 12582916
Sparse Core Ops, SparseCore 0:
  221.7 334.8 all-reduce.3

commit v2 on v1

v2 whole, which is shorter than its diff:
```python
import functools
import math

import jax
import jax.numpy as jnp
from jax import lax
from jax.experimental import pallas as pl
from jax.experimental.pallas import tpu as pltpu
from jax.sharding import PartitionSpec as P

KERNEL = 9
DILATION = 32
REACH = DILATION * (KERNEL // 2)
TILE_ROWS = 512
FF_TILE = 512
EPS = 1e-05
VMEM_BYTES = 63 * 2**20
MESH = pl.DeviceIdType.MESH
RING = 4


def passed_along(shard, axis, by):
    size = lax.axis_size(axis)
    pairs = [(i, i + by) for i in range(size) if 0 <= i + by < size]
    return lax.ppermute(shard, axis, pairs)


def product(left, right, over_left, over_right):
    return lax.dot_general(
        left, right, (((over_left,), (over_right,)), ((), ())), preferred_element_type=jnp.float32
    )


def dot(left, right):
    return product(left, right, 1, 0)


def dot_nt(left, right):
    return product(left, right, 1, 1)


def dot_tn(left, right):
    return product(left, right, 0, 0)


def gelu_parts(values):
    cumulative = 0.5 + 0.5 * lax.erf(values * (1.0 / math.sqrt(2.0)))
    density = jnp.exp(-0.5 * values * values) * (1.0 / math.sqrt(2.0 * math.pi))
    return values * cumulative, cumulative + values * density


def normalize(values):
    center = jnp.mean(values, axis=-1, keepdims=True)
    centered = values - center
    inverse = lax.rsqrt(jnp.mean(centered * centered, axis=-1, keepdims=True) + EPS)
    return centered * inverse, inverse


def normalize_back(upstream, normed, inverse, gain):
    inner = upstream * gain
    return inverse * (
        inner
        - jnp.mean(inner, axis=-1, keepdims=True)
        - normed * jnp.mean(inner * normed, axis=-1, keepdims=True)
    )


def col_sum(values):
    return jnp.sum(values, axis=0, keepdims=True)


def remote(src, dst, send_sem, recv_sem, device):
    return pltpu.make_async_remote_copy(
        src_ref=src,
        dst_ref=dst,
        send_sem=send_sem,
        recv_sem=recv_sem,
        device_id=device,
        device_id_type=MESH,
    )


def block_compute(step, depth, keeps, parts, refs):
    (
        cot,
        conv_w,
        conv_b,
        gain1,
        bias1,
        up_w,
        up_b,
        down_w,
        down_b,
        gain2,
        bias2,
        out,
        ext,
        pre_out,
        mid_out,
        d_ffn,
        d_vec,
        hidden,
        slope,
    ) = refs
    pieces = 2 * depth + 1
    group, rows_here, width = cot.shape
    rows = group * rows_here
    ff = up_w.shape[1]
    tile = min(FF_TILE, ff)
    tiles = ff // tile
    base = depth * rows_here - REACH

    @pl.when(step == 0)
    def _():
        d_ffn[...] = jnp.zeros_like(d_ffn)
        d_vec[...] = jnp.zeros_like(d_vec)

    keep_here = []
    for g in range(group):
        window = step * group + g
        for i in range(pieces):
            keep = keeps[i, window]
            if i == depth:
                keep_here.append(keep)
            ext[g, i * rows_here : (i + 1) * rows_here, :] = parts[i][g] * keep.astype(jnp.bfloat16)

    pre = jnp.broadcast_to(conv_b[...], (rows, width))
    for tap in range(KERNEL):
        begin = base + tap * DILATION
        taken = ext[:, begin : begin + rows_here, :].reshape(rows, width)
        pre = pre + dot(taken, conv_w[tap])
    act, slope1 = gelu_parts(pre)
    n1, s1 = normalize(act)
    branch = (n1 * gain1[...] + bias1[...]).astype(jnp.bfloat16)
    start = ext[:, depth * rows_here : (depth + 1) * rows_here, :].reshape(rows, width)
    middle = start.astype(jnp.float32) + branch.astype(jnp.float32)
    middle_low = middle.astype(jnp.bfloat16)

    lower = jnp.broadcast_to(down_b[...], (rows, width))
    for j in range(tiles):
        cols = slice(j * tile, (j + 1) * tile)
        upper = dot(middle_low, up_w[:, cols]) + up_b[:, cols]
        h, sl = gelu_parts(upper)
        h = h.astype(jnp.bfloat16)
        hidden[:, cols] = h
        slope[:, cols] = sl
        lower = lower + dot(h, down_w[cols, :])
    n2, s2 = normalize(lower)
    shaped = (n2 * gain2[...] + bias2[...] + middle).reshape(group, rows_here, width)
    incoming = []
    for g in range(group):
        out[g] = (shaped[g] * keep_here[g]).astype(jnp.bfloat16)
        incoming.append(cot[g].astype(jnp.float32) * keep_here[g])
    incoming = jnp.concatenate(incoming, axis=0)
    d_vec[0:1, :] += col_sum(incoming * n2)
    d_vec[1:2, :] += col_sum(incoming)
    lower_low = normalize_back(incoming, n2, s2, gain2[...]).astype(jnp.bfloat16)
    d_vec[2:3, :] += col_sum(lower_low.astype(jnp.float32))
    middle_grad = incoming
    for j in range(tiles):
        cols = slice(j * tile, (j + 1) * tile)
        hidden_grad = dot_nt(lower_low, down_w[cols, :])
        upper_low = (hidden_grad * slope[:, cols]).astype(jnp.bfloat16)
        d_vec[8 + j : 9 + j, :] += col_sum(upper_low.astype(jnp.float32))
        d_ffn[tiles + j] += dot_tn(hidden[:, cols], lower_low)
        d_ffn[j] += dot_tn(middle_low, upper_low)
        middle_grad = middle_grad + dot_nt(upper_low, up_w[:, cols])
    branch_low = middle_grad.astype(jnp.bfloat16)
    mid_out[...] = branch_low.reshape(group, rows_here, width)
    branch_grad = branch_low.astype(jnp.float32)
    d_vec[3:4, :] += col_sum(branch_grad * n1)
    d_vec[4:5, :] += col_sum(branch_grad)
    pre_low = (normalize_back(branch_grad, n1, s1, gain1[...]) * slope1).astype(jnp.bfloat16)
    d_vec[5:6, :] += col_sum(pre_low.astype(jnp.float32))
    pre_low = pre_low.reshape(group, rows_here, width)
    pre_out[...] = pre_low
    return pre_low


def block_kernel(depth, *refs):
    pieces = 2 * depth + 1
    block_compute(pl.program_id(0), depth, refs[0], refs[1 : 1 + pieces], refs[1 + pieces :])


def block_halo_kernel(steps, *refs):
    keeps, x_hbm, x_mid = refs[:3]
    inner = list(refs[3 : 3 + 15])
    pre_l, pre_r = refs[18:20]
    d_ffn, d_vec = refs[20:22]
    hidden, slope, from_l, from_r, pre_keep, fs, fr, bs, br = refs[22:]
    cot = inner[0]
    group = cot.shape[0]
    step = pl.program_id(0)
    s = lax.axis_index("seq")
    b = lax.axis_index("batch")
    last = lax.axis_size("seq") - 1
    has = (s > 0, s < last)
    other = ((s - 1, b), (s + 1, b))

    def halo(i, side):
        rows = pl.ds(i * group, group)
        land = (from_r, from_l)[side]
        return remote(x_hbm.at[rows], land.at[rows], fs.at[i, side], fr.at[i, side], other[side])

    def halo_in(i, side):
        rows = pl.ds(i * group, group)
        land = (from_l, from_r)[side]
        return remote(x_hbm.at[rows], land.at[rows], fs.at[i, side], fr.at[i, 1 - side], other[side])

    def back(i, side):
        rows = pl.ds(i * group, group)
        land = (pre_r, pre_l)[side]
        return remote(pre_keep.at[lax.rem(i, 2)], land.at[rows], bs.at[i, side], br.at[i, side], other[side])

    def back_in(i, side):
        rows = pl.ds(i * group, group)
        land = (pre_l, pre_r)[side]
        return remote(pre_keep.at[lax.rem(i, 2)], land.at[rows], bs.at[i, side], br.at[i, 1 - side], other[side])

    @pl.when(step == 0)
    def _():
        barrier = pltpu.get_barrier_semaphore()
        for side in range(2):

            @pl.when(has[side])
            def _():
                pl.semaphore_signal(barrier, inc=1, device_id=other[side], device_id_type=MESH)

        pl.semaphore_wait(barrier, (s > 0).astype(jnp.int32) + (s < last).astype(jnp.int32))
        for side in range(2):

            @pl.when(has[side])
            def _():
                halo(0, side).start()

            @pl.when(jnp.logical_not(has[side]))
            def _():
                land = (from_l, from_r)[side]
                land[...] = jnp.zeros_like(land)

    for side in range(2):

        @pl.when(has[side])
        def _():
            halo_in(step, side).wait_recv()

            @pl.when(step + 1 < steps)
            def _():
                halo(step + 1, side).start()

    rows = pl.ds(step * group, group)
    parts = (from_l.at[rows], x_mid, from_r.at[rows])
    refs_in = inner[:11] + inner[11:15] + [d_ffn, d_vec, hidden, slope]
    pre_low = block_compute(step, 1, keeps, parts, refs_in)
    for side in range(2):

        @pl.when(has[side] & (step >= 2))
        def _():
            back(step - 2, side).wait_send()

    pre_keep[lax.rem(step, 2)] = pre_low
    for side in range(2):

        @pl.when(has[side])
        def _():
            back(step, side).start()

    @pl.when(step == steps - 1)
    def _():
        for side in range(2):

            @pl.when(has[side])
            def _():
                for i in range(steps):
                    halo(i, side).wait_send()
                    back_in(i, side).wait_recv()
                for i in range(max(0, steps - 2), steps):
                    back(i, side).wait_send()


def block_params(conv_w, conv_b, gain1, bias1, up_w, up_b, down_w, down_b, gain2, bias2):
    row = lambda v: v.reshape(1, -1)
    return [conv_w, row(conv_b), row(gain1), row(bias1), up_w, row(up_b), down_w, row(down_b), row(gain2), row(bias2)]


def blocks_halo(keeps, x, cot, params):
    windows, rows_here, width = cot.shape
    ff = params[4].shape[1]
    group = TILE_ROWS // rows_here
    steps = windows // group
    rows = group * rows_here
    tile = pl.BlockSpec((group, rows_here, width), lambda i: (i, 0, 0))
    wide = pl.BlockSpec((group, 3 * rows_here, width), lambda i: (i, 0, 0))
    whole = pl.BlockSpec(memory_space=pltpu.VMEM)
    anywhere = pl.BlockSpec(memory_space=pl.ANY)
    like = jax.ShapeDtypeStruct(cot.shape, jnp.bfloat16)
    return pl.pallas_call(
        functools.partial(block_halo_kernel, steps),
        grid=(steps,),
        in_specs=[pl.BlockSpec(memory_space=pltpu.SMEM), anywhere, tile, tile] + [whole] * len(params),
        out_specs=[tile, wide, tile, tile, anywhere, anywhere, whole, whole],
        out_shape=[
            like,
            jax.ShapeDtypeStruct((windows, 3 * rows_here, width), jnp.bfloat16),
            like,
            like,
            like,
            like,
            jax.ShapeDtypeStruct((2 * ff // FF_TILE, width, FF_TILE), jnp.float32),
            jax.ShapeDtypeStruct((16, width), jnp.float32),
        ],
        scratch_shapes=[
            pltpu.VMEM((rows, ff), jnp.bfloat16),
            pltpu.VMEM((rows, ff), jnp.float32),
            pltpu.VMEM(cot.shape, jnp.bfloat16),
            pltpu.VMEM(cot.shape, jnp.bfloat16),
            pltpu.VMEM((2, group, rows_here, width), jnp.bfloat16),
            pltpu.SemaphoreType.DMA((steps, 2)),
            pltpu.SemaphoreType.DMA((steps, 2)),
            pltpu.SemaphoreType.DMA((steps, 2)),
            pltpu.SemaphoreType.DMA((steps, 2)),
        ],
        compiler_params=pltpu.CompilerParams(
            vmem_limit_bytes=VMEM_BYTES, collective_id=0, has_side_effects=True
        ),
        name="block",
    )(keeps, x, x, cot, *params)


def blocks(keeps, parts, cot, params):
    windows, rows_here, width = cot.shape
    depth = len(parts) // 2
    ff = params[4].shape[1]
    group = max(1, TILE_ROWS // rows_here)
    rows = group * rows_here
    tile = pl.BlockSpec((group, rows_here, width), lambda i: (i, 0, 0))
    wide = pl.BlockSpec((group, (2 * depth + 1) * rows_here, width), lambda i: (i, 0, 0))
    whole = pl.BlockSpec(memory_space=pltpu.VMEM)
    like = jax.ShapeDtypeStruct(cot.shape, jnp.bfloat16)
    return pl.pallas_call(
        functools.partial(block_kernel, depth),
        grid=(windows // group,),
        in_specs=[pl.BlockSpec(memory_space=pltpu.SMEM)] + [tile] * (len(parts) + 1) + [whole] * len(params),
        out_specs=[tile, wide, tile, tile, whole, whole],
        out_shape=[
            like,
            jax.ShapeDtypeStruct((windows, (2 * depth + 1) * rows_here, width), jnp.bfloat16),
            like,
            like,
            jax.ShapeDtypeStruct((2 * ff // FF_TILE, width, FF_TILE), jnp.float32),
            jax.ShapeDtypeStruct((16, width), jnp.float32),
        ],
        scratch_shapes=[pltpu.VMEM((rows, ff), jnp.bfloat16), pltpu.VMEM((rows, ff), jnp.float32)],
        compiler_params=pltpu.CompilerParams(vmem_limit_bytes=VMEM_BYTES),
        name="block_general",
    )(keeps, *parts, cot, *params)


def back_kernel(depth, *refs):
    pieces = 2 * depth + 1
    keeps = refs[0]
    parts = refs[1 : 1 + pieces]
    start_in, mid_in, conv_w, out, d_conv, ext = refs[1 + pieces :]
    step = pl.program_id(0)
    group, rows_here, width = start_in.shape
    rows = group * rows_here
    base = depth * rows_here - REACH

    @pl.when(step == 0)
    def _():
        d_conv[...] = jnp.zeros_like(d_conv)

    start = []
    for g in range(group):
        start.append(start_in[g] * keeps[depth, step * group + g].astype(jnp.bfloat16))
        for i in range(pieces):
            ext[g, i * rows_here : (i + 1) * rows_here, :] = parts[i][g]
    start = jnp.concatenate(start, axis=0)
    grad = jnp.zeros((rows, width), jnp.float32)
    for tap in range(KERNEL):
        begin = base + (KERNEL - 1 - tap) * DILATION
        taken = ext[:, begin : begin + rows_here, :].reshape(rows, width)
        d_conv[tap] += dot_tn(start, taken)
        grad = grad + dot_nt(taken, conv_w[tap])
    grad = grad.astype(jnp.bfloat16).astype(jnp.float32) + mid_in[...].reshape(rows, width).astype(jnp.float32)
    grad = grad.reshape(group, rows_here, width)
    for g in range(group):
        out[g] = (grad[g] * keeps[depth, step * group + g]).astype(jnp.bfloat16)


def conv_back(keeps, parts, start, mid, conv_w):
    windows, rows_here, width = start.shape
    depth = len(parts) // 2
    group = max(1, TILE_ROWS // rows_here)
    tile = pl.BlockSpec((group, rows_here, width), lambda i: (i, 0, 0))
    whole = pl.BlockSpec(memory_space=pltpu.VMEM)
    return pl.pallas_call(
        functools.partial(back_kernel, depth),
        grid=(windows // group,),
        in_specs=[pl.BlockSpec(memory_space=pltpu.SMEM)] + [tile] * (len(parts) + 2) + [whole],
        out_specs=[tile, whole],
        out_shape=[
            jax.ShapeDtypeStruct(start.shape, jnp.bfloat16),
            jax.ShapeDtypeStruct((KERNEL, width, width), jnp.float32),
        ],
        scratch_shapes=[pltpu.VMEM((group, (2 * depth + 1) * rows_here, width), jnp.bfloat16)],
        compiler_params=pltpu.CompilerParams(vmem_limit_bytes=VMEM_BYTES),
        name="conv_back_general",
    )(keeps, *parts, start, mid, conv_w)


class Reducer:
    stages = 8

    def __init__(self, count, acc, res, res_out, bufs, sems):
        self.count, self.acc, self.res, self.res_out = count, acc, res, res_out
        self.core_in, self.send1, self.recv1, self.kept1 = bufs[:4]
        self.send2, self.recv2, self.kept2 = bufs[4:7]
        self.send3, self.recv3, self.kept3, self.fin = bufs[7:11]
        (
            self.c_s, self.c_r, self.a_s, self.a_r, self.b_s, self.b_r, self.z_s, self.z_r,
            self.zg_s, self.zg_r, self.bg_s, self.bg_r, self.ag_s, self.ag_r, self.cg_s, self.cg_r, self.out_s,
        ) = sems
        s, b = lax.axis_index("seq"), lax.axis_index("batch")
        self.core, self.z = lax.rem(s, 2), lax.div(s, 2)
        self.x, self.y = lax.rem(b, 2), lax.div(b, 2)
        self.core_peer = (s + 1 - 2 * self.core, b)
        x_peer = (s, b + 1 - 2 * self.x)
        y_peer = (s, b + 2 - 4 * self.y)
        self.first_peer, self.second_peer = (x_peer, y_peer), (y_peer, x_peer)
        self.z_to = [(lax.rem(self.z + d, 4) * 2 + self.core, b) for d in (1, 2, 3)]
        self.z_of = [lax.rem(self.z + d, 4) for d in (1, 2, 3)]
        self.first, self.second = (self.x, self.y), (self.y, self.x)
        self.half = acc.shape[1] // 2
        self.own = self.core * self.half
        self.cols = (slice(0, 256), slice(256, 512))
        self.vec_peers = [
            self.core_peer,
            x_peer,
            y_peer,
            (s + 2 - 4 * lax.rem(self.z, 2), b),
            (s + 4 - 8 * lax.div(self.z, 2), b),
        ]

    def peers(self):
        return [self.core_peer, self.first_peer[0], self.first_peer[1]] + self.z_to

    def rows(self, base, count):
        return pl.ds(pl.multiple_of(base, 16), count)

    def core_copy(self, c):
        r = lax.rem(c, RING)
        away = self.rows((1 - self.core) * self.half, self.half)
        return remote(self.acc.at[r, away], self.core_in.at[r], self.c_s.at[r], self.c_r.at[r], self.core_peer)

    def copy1(self, c, h):
        r = lax.rem(c, RING)
        at = (r, slice(None), self.cols[h])
        return remote(self.send1.at[at], self.recv1.at[at], self.a_s.at[r, h], self.a_r.at[r, h], self.first_peer[h])

    def copy2(self, c, h):
        r = lax.rem(c, RING)
        at = (r, slice(None), self.cols[h])
        return remote(self.send2.at[at], self.recv2.at[at], self.b_s.at[r, h], self.b_r.at[r, h], self.second_peer[h])

    def copy3(self, c, d):
        r = lax.rem(c, RING)
        return remote(self.send3.at[r, d], self.recv3.at[r, d], self.z_s.at[r, d], self.z_r.at[r, d], self.z_to[d])

    def base1(self, h):
        return self.own + self.first[h] * 128

    def base2(self, h):
        return self.base1(h) + self.second[h] * 64

    def spread_z(self, c, d, h):
        r = lax.rem(c, RING)
        land = self.res.at[c, self.rows(self.base2(h) + self.z * 16, 16), self.cols[h]]
        return remote(
            self.fin.at[r, :, self.cols[h]], land, self.zg_s.at[r, d, h], self.zg_r.at[r, d, h], self.z_to[d]
        )

    def spread_same(self, c, base, count, cols, s, r, peer):
        part = self.res.at[c, self.rows(base, count), cols]
        return remote(part, part, s, r, peer)

    def spread2(self, c, h):
        r = lax.rem(c, RING)
        return self.spread_same(
            c, self.base2(h), 64, self.cols[h], self.bg_s.at[r, h], self.bg_r.at[r, h], self.second_peer[h]
        )

    def spread1(self, c, h):
        r = lax.rem(c, RING)
        return self.spread_same(
            c, self.base1(h), 128, self.cols[h], self.ag_s.at[r, h], self.ag_r.at[r, h], self.first_peer[h]
        )

    def spread_core(self, c):
        r = lax.rem(c, RING)
        return self.spread_same(
            c, self.own, self.half, slice(0, 512), self.cg_s.at[r], self.cg_r.at[r], self.core_peer
        )

    def write_out(self, c, act):
        up_out, down_out, conv_out = self.res_out
        width, tiles = self.acc.shape[1], up_out.shape[1] // self.acc.shape[1]
        wide = lambda i: pl.ds(pl.multiple_of(i * width, width), width)

        def copy(to):
            return lambda: act(pltpu.make_async_copy(self.res.at[c], to, self.out_s.at[lax.rem(c, 2)]))

        pl.when(c < tiles)(copy(up_out.at[:, wide(c)]))
        pl.when((c >= tiles) & (c < 2 * tiles))(copy(down_out.at[wide(c - tiles), :]))
        pl.when(c >= 2 * tiles)(copy(conv_out.at[c - 2 * tiles]))

    def stage0(self, c):
        self.core_copy(c).start()

    def stage1(self, c):
        self.core_copy(c).wait()
        r = lax.rem(c, RING)
        for h in range(2):
            cols = self.cols[h]
            keep, give = self.first[h] * 128, (1 - self.first[h]) * 128
            self.send1[r, :, cols] = (
                self.acc[r, self.rows(self.own + give, 128), cols] + self.core_in[r, self.rows(give, 128), cols]
            ).astype(jnp.bfloat16)
            self.copy1(c, h).start()
            self.kept1[r, :, cols] = (
                self.acc[r, self.rows(self.own + keep, 128), cols] + self.core_in[r, self.rows(keep, 128), cols]
            )

    def stage2(self, c):
        r = lax.rem(c, RING)
        for h in range(2):
            self.copy1(c, h).wait()
            cols = self.cols[h]
            keep, give = self.second[h] * 64, (1 - self.second[h]) * 64
            self.send2[r, :, cols] = (
                self.kept1[r, self.rows(give, 64), cols]
                + self.recv1[r, self.rows(give, 64), cols].astype(jnp.float32)
            ).astype(jnp.bfloat16)
            self.copy2(c, h).start()
            self.kept2[r, :, cols] = self.kept1[r, self.rows(keep, 64), cols] + self.recv1[
                r, self.rows(keep, 64), cols
            ].astype(jnp.float32)

    def stage3(self, c):
        r = lax.rem(c, RING)
        for h in range(2):
            self.copy2(c, h).wait()
        for d in range(3):
            at = self.rows(self.z_of[d] * 16, 16)
            self.send3[r, d] = (self.kept2[r, at, :] + self.recv2[r, at, :].astype(jnp.float32)).astype(jnp.bfloat16)
            self.copy3(c, d).start()
        at = self.rows(self.z * 16, 16)
        self.kept3[r] = self.kept2[r, at, :] + self.recv2[r, at, :].astype(jnp.float32)

    def stage4(self, c):
        r = lax.rem(c, RING)
        total = self.kept3[r]
        for d in range(3):
            self.copy3(c, d).wait()
            total = total + self.recv3[r, d].astype(jnp.float32)
        total = total.astype(jnp.bfloat16)
        self.fin[r] = total
        for h in range(2):
            for d in range(3):
                self.spread_z(c, d, h).start()
            self.res[c, self.rows(self.base2(h) + self.z * 16, 16), self.cols[h]] = total[:, self.cols[h]]

    def stage5(self, c):
        for h in range(2):
            for d in range(3):
                self.spread_z(c, d, h).wait()
            self.spread2(c, h).start()

    def stage6(self, c):
        for h in range(2):
            self.spread2(c, h).wait()
            self.spread1(c, h).start()

    def stage7(self, c):
        for h in range(2):
            self.spread1(c, h).wait()
        self.spread_core(c).start()

    def stage8(self, c):
        self.spread_core(c).wait()

        @pl.when(c >= 2)
        def _():
            self.write_out(c - 2, lambda copy: copy.wait())

        self.write_out(c, lambda copy: copy.start())

    def tick(self, t):
        for stage in range(self.stages, -1, -1):
            c = t - stage

            @pl.when((c >= 0) & (c < self.count))
            def _():
                getattr(self, "stage%d" % stage)(c)

    def finish(self):
        for c in range(max(0, self.count - 2), self.count):
            self.write_out(jnp.int32(c), lambda copy: copy.wait())


def reduce_kernel(steps, *refs):
    (
        keeps, ffn, vec_in, ext_hbm, pre_hbm, pre_l, pre_r, mid_hbm, conv_w,
        grad_out, up_out, down_out, conv_out, vec_out,
        ext, pre, acc, res, pext, midb, gout, vsend, vrecv,
    ) = refs[:23]
    bufs = refs[23:34]
    sems = refs[34:51]
    load_s, ffn_s, in_s, gout_s, v_s, v_r = refs[51:]
    ffn_count = ffn.shape[0]
    count = ffn_count + KERNEL
    group, rows_here, width = gout.shape[1:]
    rows = group * rows_here
    red = Reducer(count, acc, res, (up_out, down_out, conv_out), bufs, sems)
    s = lax.axis_index("seq")
    last = lax.axis_size("seq") - 1

    barrier = pltpu.get_barrier_semaphore()
    for peer in red.peers():
        pl.semaphore_signal(barrier, inc=1, device_id=peer, device_id_type=MESH)

    load_ext = pltpu.make_async_copy(ext_hbm, ext, load_s.at[0])
    load_pre = pltpu.make_async_copy(pre_hbm, pre, load_s.at[1])

    def load_ffn(c):
        r = lax.rem(c, RING)
        return pltpu.make_async_copy(ffn.at[c], acc.at[r], ffn_s.at[r])

    def load_rows(i):
        slot = lax.rem(i, 2)
        at = pl.ds(i * group, group)
        return (
            pltpu.make_async_copy(pre_l.at[at], pext.at[slot, :, pl.ds(0, rows_here)], in_s.at[slot, 0]),
            pltpu.make_async_copy(pre_hbm.at[at], pext.at[slot, :, pl.ds(rows_here, rows_here)], in_s.at[slot, 1]),
            pltpu.make_async_copy(pre_r.at[at], pext.at[slot, :, pl.ds(2 * rows_here, rows_here)], in_s.at[slot, 2]),
            pltpu.make_async_copy(mid_hbm.at[at], midb.at[slot], in_s.at[slot, 3]),
        )

    def each_load(i, act):
        a, m, z, d = load_rows(i)
        pl.when(s > 0)(lambda: act(a))
        act(m)
        pl.when(s < last)(lambda: act(z))
        act(d)

    def store_rows(i):
        slot = lax.rem(i, 2)
        return pltpu.make_async_copy(gout.at[slot], grad_out.at[pl.ds(i * group, group)], gout_s.at[slot])

    load_ffn(0).start()
    each_load(0, lambda copy: copy.start())
    load_ext.start()
    load_pre.start()
    for side, at in ((s > 0, 0), (s < last, 2)):

        @pl.when(jnp.logical_not(side))
        def _():
            pext[:, :, at * rows_here : (at + 1) * rows_here, :] = jnp.zeros(
                (2, group, rows_here, width), jnp.bfloat16
            )

    pl.semaphore_wait(barrier, len(red.peers()))

    def vec_copy(q):
        return remote(vsend.at[q], vrecv.at[q], v_s.at[q], v_r.at[q], red.vec_peers[q])

    def row_block(i):
        each_load(i, lambda copy: copy.wait())

        @pl.when(i + 1 < steps)
        def _():
            each_load(i + 1, lambda copy: copy.start())

        slot = lax.rem(i, 2)
        grad = jnp.zeros((rows, width), jnp.float32)
        for tap in range(KERNEL):
            begin = (KERNEL - 1 - tap) * DILATION
            taken = pext[slot, :, begin : begin + rows_here, :].reshape(rows, width)
            grad = grad + dot_nt(taken, conv_w[tap])
        grad = grad.astype(jnp.bfloat16).astype(jnp.float32)
        grad = (grad + midb[slot].reshape(rows, width).astype(jnp.float32)).reshape(group, rows_here, width)

        @pl.when(i >= 2)
        def _():
            store_rows(i - 2).wait()

        for g in range(group):
            gout[slot, g] = (grad[g] * keeps[1, i * group + g]).astype(jnp.bfloat16)
        store_rows(i).start()

    def tap_grad(tap):
        r = lax.rem(ffn_count + tap, RING)
        begin = pl.multiple_of(tap * DILATION, DILATION)

        def part(i, first):
            at = pl.ds(i * 2 * group, 2 * group)
            taken = ext[at, pl.ds(begin, rows_here), :].reshape(2 * rows, width)
            grads = pre[at].reshape(2 * rows, width)
            value = dot_tn(taken, grads)
            acc[r] = value if first else acc[r] + value

        part(0, True)
        lax.fori_loop(1, steps // 2, lambda i, _: (part(i, False), 0)[1], 0)

    def tick(t, _):
        @pl.when(t < ffn_count)
        def _():
            load_ffn(t).wait()

        red.tick(t)
        for q in range(6):

            @pl.when(t == q)
            def _():
                if q == 0:
                    value = vec_in[...]
                else:
                    vec_copy(q - 1).wait()
                    value = vsend[q - 1] + vrecv[q - 1]
                if q < 5:
                    vsend[q] = value
                    vec_copy(q).start()
                else:
                    vec_out[...] = value

        @pl.when(t + 1 < ffn_count)
        def _():
            load_ffn(t + 1).start()

        @pl.when(t < steps)
        def _():
            row_block(t)

        @pl.when(t == ffn_count - 1)
        def _():
            load_ext.wait()
            load_pre.wait()

        tap = t + 1 - ffn_count

        @pl.when((tap >= 0) & (tap < KERNEL))
        def _():
            tap_grad(tap)

        return 0

    lax.fori_loop(0, count + red.stages, tick, 0)
    red.finish()
    for i in range(max(0, steps - 2), steps):
        store_rows(i).wait()


def reduce_all(keeps, ffn, vec, ext, pre, pre_l, pre_r, mid, conv_w):
    windows, rows_here, width = pre.shape
    group = TILE_ROWS // rows_here
    steps = windows // group
    count = ffn.shape[0] + KERNEL
    whole = pl.BlockSpec(memory_space=pltpu.VMEM)
    anywhere = pl.BlockSpec(memory_space=pl.ANY)
    dma = pltpu.SemaphoreType.DMA
    half = width // 2
    return pl.pallas_call(
        functools.partial(reduce_kernel, steps),
        in_specs=[pl.BlockSpec(memory_space=pltpu.SMEM), anywhere, whole] + [anywhere] * 5 + [whole],
        out_specs=[anywhere] * 4 + [whole],
        out_shape=[
            jax.ShapeDtypeStruct(pre.shape, jnp.bfloat16),
            jax.ShapeDtypeStruct((width, ffn.shape[0] // 2 * width), jnp.bfloat16),
            jax.ShapeDtypeStruct((ffn.shape[0] // 2 * width, width), jnp.bfloat16),
            jax.ShapeDtypeStruct((KERNEL, width, width), jnp.bfloat16),
            jax.ShapeDtypeStruct(vec.shape, jnp.float32),
        ],
        scratch_shapes=[
            pltpu.VMEM(ext.shape, jnp.bfloat16),
            pltpu.VMEM(pre.shape, jnp.bfloat16),
            pltpu.VMEM((RING, width, width), jnp.float32),
            pltpu.VMEM((count, width, width), jnp.bfloat16),
            pltpu.VMEM((2, group, 3 * rows_here, width), jnp.bfloat16),
            pltpu.VMEM((2, group, rows_here, width), jnp.bfloat16),
            pltpu.VMEM((2, group, rows_here, width), jnp.bfloat16),
            pltpu.VMEM((5,) + vec.shape, jnp.float32),
            pltpu.VMEM((5,) + vec.shape, jnp.float32),
            pltpu.VMEM((RING, half, width), jnp.float32),
            pltpu.VMEM((RING, half // 2, width), jnp.bfloat16),
            pltpu.VMEM((RING, half // 2, width), jnp.bfloat16),
            pltpu.VMEM((RING, half // 2, width), jnp.float32),
            pltpu.VMEM((RING, half // 4, width), jnp.bfloat16),
            pltpu.VMEM((RING, half // 4, width), jnp.bfloat16),
            pltpu.VMEM((RING, half // 4, width), jnp.float32),
            pltpu.VMEM((RING, 3, half // 16, width), jnp.bfloat16),
            pltpu.VMEM((RING, 3, half // 16, width), jnp.bfloat16),
            pltpu.VMEM((RING, half // 16, width), jnp.float32),
            pltpu.VMEM((RING, half // 16, width), jnp.bfloat16),
        ]
        + [
            dma((RING,)), dma((RING,)), dma((RING, 2)), dma((RING, 2)), dma((RING, 2)), dma((RING, 2)),
            dma((RING, 3)), dma((RING, 3)), dma((RING, 3, 2)), dma((RING, 3, 2)), dma((RING, 2)), dma((RING, 2)),
            dma((RING, 2)), dma((RING, 2)), dma((RING,)), dma((RING,)), dma((2,)),
        ]
        + [dma((2,)), dma((RING,)), dma((2, 4)), dma((2,)), dma((5,)), dma((5,))],
        compiler_params=pltpu.CompilerParams(
            vmem_limit_bytes=VMEM_BYTES, collective_id=1, has_side_effects=True
        ),
        name="reduce",
    )(keeps, ffn, vec, ext, pre, pre_l, pre_r, mid, conv_w)


def spread(shard, depth):
    return [
        shard if offset == 0 else passed_along(shard, "seq", offset)
        for offset in range(depth, -depth - 1, -1)
    ]


def per_device(
    block_input,
    window_lengths,
    conv_weight,
    conv_bias,
    norm1_gain,
    norm1_bias,
    up_weight,
    up_bias,
    down_weight,
    down_bias,
    norm2_gain,
    norm2_bias,
    out_cotangent,
):
    windows, rows_here, width = block_input.shape
    ff = up_weight.shape[1]
    depth = -(-REACH // rows_here)
    first = (lax.axis_index("seq") + jnp.arange(-depth, depth + 1, dtype=jnp.int32)) * rows_here
    keeps = (first[:, None] < window_lengths[None, :]).astype(jnp.float32)
    params = block_params(
        conv_weight, conv_bias, norm1_gain, norm1_bias, up_weight, up_bias, down_weight, down_bias, norm2_gain, norm2_bias
    )
    tiles = ff // FF_TILE
    if (lax.axis_size("seq"), lax.axis_size("batch"), rows_here) == (8, 4, REACH):
        out, ext, pre_low, mid_low, pre_l, pre_r, d_ffn, d_vec = blocks_halo(keeps, block_input, out_cotangent, params)
        input_grad, d_up, d_down, d_conv, d_vec = reduce_all(
            keeps, d_ffn, d_vec, ext, pre_low, pre_l, pre_r, mid_low, conv_weight
        )
        d_up, d_down, d_conv = (d.astype(jnp.float32) for d in (d_up, d_down, d_conv))
    else:
        parts = spread(block_input, depth)
        out, _, pre_low, mid_low, d_ffn, d_vec = blocks(keeps, parts, out_cotangent, params)
        input_grad, d_conv = conv_back(keeps, spread(pre_low, depth), block_input, mid_low, conv_weight)
        d_ffn, d_conv, d_vec = lax.psum((d_ffn, d_conv, d_vec), ("seq", "batch"))
        d_up = d_ffn[:tiles].transpose(1, 0, 2).reshape(width, ff)
        d_down = d_ffn[tiles:].reshape(ff, width)
    return (
        out,
        input_grad,
        d_conv,
        d_vec[5],
        d_vec[3],
        d_vec[4],
        d_up,
        d_vec[8 : 8 + tiles].reshape(ff),
        d_down,
        d_vec[2],
        d_vec[0],
        d_vec[1],
    )


def solution(mesh):
    rows = P("batch", "seq", None)
    return jax.shard_map(
        per_device,
        mesh=mesh,
        in_specs=(rows, P("batch")) + (P(),) * 10 + (rows,),
        out_specs=(rows, rows) + (P(),) * 10,
        check_vma=False,
    )
```

time: 580 us -> 269 us (0.46)
  waiting for transfers between devices: 251 us -> 0 us
  Pallas kernels: 149 us -> 244 us
  blocking collectives: 83.1 us -> 0 us
  starting transfers between devices: 51.8 us -> 0 us
  local copies, waits for them, and re-layouts: 30.3 us -> 9.91 us
  between operations: 14.1 us -> 0.69 us
  other arithmetic: 0.65 us -> 13.3 us
    psum x1 -> x0, waiting for transfers between devices: 251 us -> none  [per_device(): lax.psum((d_conv, d_up, d_down_t, d_vec, d_upb), ('seq', 'batch'))]
    pallas_call x2, Pallas kernels: 149 us -> 244 us  [the longest x1 125 us: reduce_all(): pl.pallas_call(functools.partial(reduce_kernel, steps), in_specs=[pl.Bloc...]
    psum x1 -> x0, blocking collectives: 83.1 us -> none  [per_device(): lax.psum((d_conv, d_up, d_down_t, d_vec, d_upb), ('seq', 'batch'))]
    ppermute x4 -> x0, starting transfers between devices: 51.8 us -> none  [passed_along(): return lax.ppermute(shard, axis, pairs)]
    unnamed x16 -> x12, local copies, waits for them, and re-layouts: 29.7 us -> 8.31 us
    convert_element_type x0 -> x3, other arithmetic: none -> 12 us  [per_device(): d.astype(jnp.float32)]
  transfers between devices with their start and end apart: 5 -> 0, of which waited for: 1 -> 0; matrix products, arithmetic and copies ran while one was open for 2% -> 0% of each run, Pallas kernels for 0% -> 0%
where the time goes in v2:
time: 269 us; the launch traced here: 268 us
  Pallas kernels  244 us (91%)
  other arithmetic  13.3 us (5%)
  local copies, waits for them, and re-layouts  9.91 us (4%)
    pallas_call x1, Pallas kernels, reduce_all(): pl.pallas_call(functools.partial(reduce_kernel, steps), in_specs=[pl.Bloc...  125 us
    pallas_call x1, Pallas kernels, blocks_halo(): pl.pallas_call(functools.partial(block_halo_kernel, steps), grid=(steps,)...  119 us
    convert_element_type x3, other arithmetic, per_device(): d.astype(jnp.float32)  12 us
    unnamed x12, local copies, waits for them, and re-layouts  8.31 us

profile of v2, /device:TPU:0, one launch (start us, length us, event | category | flops | bytes accessed | tf_op | source)
XLA Modules:
  0.0 268.3 jit_solution(6095220910853359931)
XLA Ops:
  0.7 1.3 compare_convert_fusion.refs_0_
  2.0 119.2 %block.1 = (bf16[32,128,512]{2,1,0:T(8,128)(2,1)}, bf16[32,384,512]{2,1,0:T(8,128)(2,1)}, bf16[32,128,512]{2,1,0:T(8,128)(2,1)}, bf16[32,128,512]{2,1,0:T(8,128)...) custom-call(f32[3,32]{1,0:T(4,128)} %compare_convert_fusion.refs_0_,, ...), custom_call_target="tpu_custom_call" | custom-call | tf_op jit(solution)/shard_map/block/pallas_call | solution.py:297
  121.2 125.3 %reduce.1 = (bf16[32,128,512]{2,1,0:T(8,128)(2,1)}, bf16[512,2048]{1,0:T(8,128)(2,1)}, bf16[2048,512]{1,0:T(8,128)(2,1)}, bf16[9,512,512]{2,1,0:T(8,128)(2,1)}, f32[16,512]{1,0:T(8,128)}) custom-call(f32[3,32]{1,0:T(4,128)} %compare_convert_fusion.refs_0_, f32[8,512,512]{2,1,0:T(8,128)} %get-tuple-element.26.refs_1_, f32[16,512]{1,0:T(8,128)} %get-tuple-element.27.refs_2_, ...), custom_call_target="tpu_custom_call" | custom-call | tf_op jit(solution)/shard_map/reduce/pallas_call | solution.py:772
  246.5 0.0 copy-start.3
  246.5 0.9 slice_bitcast_fusion
  247.3 1.6 fusion
  248.9 0.6 copy.25
  249.5 4.1 %convert_element_type.14 = f32[512,2048]{1,0:T(8,128)} convert(bf16[512,2048]{1,0:T(8,128)(2,1)} %get-tuple-element.36) | non-fusion elementwise | flops 1048576 | bytes 6291456 | tf_op jit(solution)/shard_map/convert_element_type | solution.py:854
  253.7 0.0 copy-done.3
  253.7 0.0 copy-start
  253.7 2.7 %convert_element_type.15 = f32[2048,512]{1,0:T(8,128)} convert(bf16[2048,512]{1,0:T(8,128)(2,1)S(1)} %copy-done.3) | non-fusion elementwise | flops 1048576 | bytes 6291456 | tf_op jit(solution)/shard_map/convert_element_type | solution.py:854
  256.4 1.1 copy-done
  257.5 0.0 copy-start.1
  257.5 5.1 %convert_element_type.13 = f32[9,512,512]{2,1,0:T(8,128)} convert(bf16[9,512,512]{2,1,0:T(8,128)(2,1)S(1)} %copy-done) | non-fusion elementwise | flops 2359296 | bytes 14155776 | tf_op jit(solution)/shard_map/convert_element_type | solution.py:854
  262.6 0.0 copy-done.1
  262.6 0.0 copy-start.2
  262.6 2.1 copy.28
  264.8 1.6 copy-done.2
  266.3 2.0 copy.29
  (1 shorter events, 0.0 us)
Async XLA Ops:
  246.5 7.2 %copy-start.3 = (bf16[2048,512]{1,0:T(8,128)(2,1)S(1)}, bf16[2048,512]{1,0:T(8,128)(2,1)}, u32[]{:S(2)}) copy-start(bf16[2048,512]{1,0:T(8,128)(2,1)} %get-tuple-element.37) | copy-start | bytes 6291460
  253.7 3.9 %copy-start = (bf16[9,512,512]{2,1,0:T(8,128)(2,1)S(1)}, bf16[9,512,512]{2,1,0:T(8,128)(2,1)}, u32[]{:S(2)}) copy-start(bf16[9,512,512]{2,1,0:T(8,128)(2,1)} %get-tuple-element.34) | copy-start | bytes 14155780
  257.5 5.1 %copy-start.1 = (bf16[32,128,512]{2,1,0:T(8,128)(2,1)S(1)}, bf16[32,128,512]{2,1,0:T(8,128)(2,1)}, u32[]{:S(2)}) copy-start(bf16[32,128,512]{2,1,0:T(8,128)(2,1)} %get-tuple-element.56) | copy-start | bytes 12582916
  262.6 3.7 %copy-start.2 = (bf16[32,128,512]{2,1,0:T(8,128)(2,1)S(1)}, bf16[32,128,512]{2,1,0:T(8,128)(2,1)}, u32[]{:S(2)}) copy-start(bf16[32,128,512]{2,1,0:T(8,128)(2,1)} %get-tuple-element.57) | copy-start | bytes 12582916

commit v3 on v2

--- a/solution.py
+++ b/solution.py
@@ -17,6 +17,8 @@
 VMEM_BYTES = 63 * 2**20
 MESH = pl.DeviceIdType.MESH
 RING = 4
+EARLY = 4
+AHEAD = 3
 
 
 def passed_along(shard, axis, by):
@@ -97,9 +99,11 @@
         ext,
         pre_out,
         mid_out,
-        d_ffn,
+        hidden,
+        upper_out,
+        lower_out,
+        middle_out,
         d_vec,
-        hidden,
         slope,
     ) = refs
     pieces = 2 * depth + 1
@@ -112,7 +116,6 @@
 
     @pl.when(step == 0)
     def _():
-        d_ffn[...] = jnp.zeros_like(d_ffn)
         d_vec[...] = jnp.zeros_like(d_vec)
 
     keep_here = []
@@ -135,6 +138,7 @@
     start = ext[:, depth * rows_here : (depth + 1) * rows_here, :].reshape(rows, width)
     middle = start.astype(jnp.float32) + branch.astype(jnp.float32)
     middle_low = middle.astype(jnp.bfloat16)
+    middle_out[...] = middle_low
 
     lower = jnp.broadcast_to(down_b[...], (rows, width))
     for j in range(tiles):
@@ -155,6 +159,7 @@
     d_vec[0:1, :] += col_sum(incoming * n2)
     d_vec[1:2, :] += col_sum(incoming)
     lower_low = normalize_back(incoming, n2, s2, gain2[...]).astype(jnp.bfloat16)
+    lower_out[...] = lower_low
     d_vec[2:3, :] += col_sum(lower_low.astype(jnp.float32))
     middle_grad = incoming
     for j in range(tiles):
@@ -162,8 +167,7 @@
         hidden_grad = dot_nt(lower_low, down_w[cols, :])
         upper_low = (hidden_grad * slope[:, cols]).astype(jnp.bfloat16)
         d_vec[8 + j : 9 + j, :] += col_sum(upper_low.astype(jnp.float32))
-        d_ffn[tiles + j] += dot_tn(hidden[:, cols], lower_low)
-        d_ffn[j] += dot_tn(middle_low, upper_low)
+        upper_out[:, cols] = upper_low
         middle_grad = middle_grad + dot_nt(upper_low, up_w[:, cols])
     branch_low = middle_grad.astype(jnp.bfloat16)
     mid_out[...] = branch_low.reshape(group, rows_here, width)
@@ -182,14 +186,39 @@
     block_compute(pl.program_id(0), depth, refs[0], refs[1 : 1 + pieces], refs[1 + pieces :])
 
 
-def block_halo_kernel(steps, *refs):
-    keeps, x_hbm, x_mid = refs[:3]
-    inner = list(refs[3 : 3 + 15])
-    pre_l, pre_r = refs[18:20]
-    d_ffn, d_vec = refs[20:22]
-    hidden, slope, from_l, from_r, pre_keep, fs, fr, bs, br = refs[22:]
-    cot = inner[0]
-    group = cot.shape[0]
+def interleave(units, pieces):
+    done = 0
+    for n, unit in enumerate(units):
+        unit()
+        upto = (n + 1) * len(pieces) // len(units)
+        for piece in pieces[done:upto]:
+            piece()
+        done = upto
+    for piece in pieces[done:]:
+        piece()
+
+
+def halves(count, size=256):
+    return [slice(k * size, (k + 1) * size) for k in range(count // size)]
+
+
+def rows_in_eights(values):
+    return jnp.sum(values.reshape(-1, 8, values.shape[-1]), axis=0)
+
+
+def block_halo_kernel(blocks, *refs):
+    (
+        keeps, x_hbm, x_mid, cot, conv_w, conv_b, gain1, bias1, up_w, up_b, down_w, down_b, gain2, bias2,
+        out_hbm, ext_hbm, pre_hbm, mid_hbm, hidden_hbm, upper_hbm, lower_hbm, middle_hbm, pre_l, pre_r, d_vec,
+        out, ext, mid_out, hidden, upper_out, lower_out,
+        slope, conv_acc, n1_all, q1_all, middle, middle_low, lower, mid_grad, vec_acc, upb_acc,
+        from_l, from_r, pre_keep, fs, fr, bs, br, ps,
+    ) = refs
+    group, rows_here, width = cot.shape
+    rows = group * rows_here
+    ff = up_w.shape[1]
+    fine, side_tile = 16, 256
+    per_side = side_tile // rows_here
     step = pl.program_id(0)
     s = lax.axis_index("seq")
     b = lax.axis_index("batch")
@@ -197,25 +226,244 @@
     has = (s > 0, s < last)
     other = ((s - 1, b), (s + 1, b))
 
-    def halo(i, side):
-        rows = pl.ds(i * group, group)
+    core = lax.rem(s, 2)
+
+    def near_first(act):
+        for side in range(2):
+            pl.when(has[1 - side] & (core == 0))(lambda side=1 - side: act(side))
+            pl.when(has[side] & (core == 1))(lambda side=side: act(side))
+
+    def place(i, part):
+        if part is None:
+            return pl.ds(i * group, group), i + 1
+        return pl.ds(part * (group // 2), group // 2), part
+
+    def halo(i, side, part=None):
+        at, k = place(i, part)
         land = (from_r, from_l)[side]
-        return remote(x_hbm.at[rows], land.at[rows], fs.at[i, side], fr.at[i, side], other[side])
-
-    def halo_in(i, side):
-        rows = pl.ds(i * group, group)
+        return remote(x_hbm.at[at], land.at[at], fs.at[k, side], fr.at[k, side], other[side])
+
+    def halo_in(i, side, part=None):
+        at, k = place(i, part)
         land = (from_l, from_r)[side]
-        return remote(x_hbm.at[rows], land.at[rows], fs.at[i, side], fr.at[i, 1 - side], other[side])
+        return remote(x_hbm.at[at], land.at[at], fs.at[k, side], fr.at[k, 1 - side], other[side])
+
+    def put(k, block):
+        at = pl.ds(block * group, group)
+        flat = pl.ds(block * rows, rows)
+        source, target = (
+            lambda: (ext, ext_hbm.at[at]),
+            lambda: (hidden, hidden_hbm.at[flat]),
+            lambda: (pre_keep.at[lax.rem(block, 2)], pre_hbm.at[at]),
+            lambda: (mid_out, mid_hbm.at[at]),
+            lambda: (out, out_hbm.at[at]),
+            lambda: (lower_out, lower_hbm.at[flat]),
+            lambda: (upper_out, upper_hbm.at[flat]),
+            lambda: (middle_low, middle_hbm.at[flat]),
+        )[k]()
+        return pltpu.make_async_copy(source, target, ps.at[k])
+
+    def puts(start, *pairs):
+        for k, block in pairs:
+
+            @pl.when((block >= 0) & (block < blocks))
+            def _():
+                if start:
+                    put(k, block).start()
+                else:
+                    put(k, block).wait()
 
     def back(i, side):
-        rows = pl.ds(i * group, group)
+        at = pl.ds(i * group, group)
         land = (pre_r, pre_l)[side]
-        return remote(pre_keep.at[lax.rem(i, 2)], land.at[rows], bs.at[i, side], br.at[i, side], other[side])
+        return remote(pre_keep.at[lax.rem(i, 2)], land.at[at], bs.at[i, side], br.at[i, side], other[side])
 
     def back_in(i, side):
-        rows = pl.ds(i * group, group)
+        at = pl.ds(i * group, group)
         land = (pre_l, pre_r)[side]
-        return remote(pre_keep.at[lax.rem(i, 2)], land.at[rows], bs.at[i, side], br.at[i, 1 - side], other[side])
+        return remote(pre_keep.at[lax.rem(i, 2)], land.at[at], bs.at[i, side], br.at[i, 1 - side], other[side])
+
+    conv_slot = lax.rem(step, 2)
+    back_slot = lax.rem(step, 2)
+    keep_slot = lax.rem(step, 2)
+    fine_rows = [slice(k * fine, (k + 1) * fine) for k in range(rows // fine)]
+    sides = halves(rows)
+    tiles = halves(ff)
+    outs = halves(width)
+
+    def add_vec(k, values):
+        vec_acc[k] += rows_in_eights(values)
+
+    def build_ext(w):
+        parts = (from_l, x_mid, from_r)
+
+        def piece():
+            for k in range(3):
+                keep = keeps[k, step * group + w].astype(jnp.bfloat16)
+                rows_of = x_mid[w] if k == 1 else parts[k][step * group + w]
+                ext[w, k * rows_here : (k + 1) * rows_here, :] = rows_of * keep
+
+        return piece
+
+    def conv_units():
+        units = []
+        for m, side in enumerate(sides):
+            for cols in outs:
+                held = {}
+
+                def unit(tap, m=m, side=side, cols=cols, held=held):
+                    def run():
+                        begin = tap * DILATION
+                        taken = ext[m * per_side : (m + 1) * per_side, begin : begin + rows_here, :]
+                        value = dot(taken.reshape(side_tile, width), conv_w[tap, :, cols])
+                        held["acc"] = value if tap == 0 else held["acc"] + value
+                        if tap == KERNEL - 1:
+                            conv_acc[side, cols] = held["acc"]
+
+                    return run
+
+                units += [unit(tap) for tap in range(KERNEL)]
+        return units
+
+    def first_norm(r):
+        def piece():
+            act, slope1 = gelu_parts(conv_acc[r, :] + conv_b[...])
+            n1, s1 = normalize(act)
+            branch = (n1 * gain1[...] + bias1[...]).astype(jnp.bfloat16)
+            w, at = r.start // rows_here, r.start % rows_here
+            start = ext[w, rows_here + at : rows_here + at + fine, :]
+            value = start.astype(jnp.float32) + branch.astype(jnp.float32)
+            middle[r, :] = value
+            low = value.astype(jnp.bfloat16)
+            middle_low[r, :] = low
+            n1_all[conv_slot, r, :] = n1
+            q1_all[conv_slot, r, :] = s1 * slope1
+
+        return piece
+
+    def forward_slots(extra):
+        ups, lowers = {}, {}
+
+        def up(j, m):
+            def run():
+                ups[j, m] = dot(middle_low[sides[m], :], up_w[:, tiles[j]])
+
+            return run
+
+        def act(j, m, k):
+            def run():
+                at = slice(k * 64, (k + 1) * 64)
+                r = slice(m * side_tile + k * 64, m * side_tile + (k + 1) * 64)
+                h, sl = gelu_parts(ups[j, m][at] + up_b[:, tiles[j]])
+                hidden[r, tiles[j]] = h.astype(jnp.bfloat16)
+                slope[r, tiles[j]] = sl
+
+            return run
+
+        def down(j, m, n):
+            def run():
+                value = dot(hidden[sides[m], tiles[j]], down_w[tiles[j], outs[n]])
+                lowers[m, n] = lowers[m, n] + value if j > 0 else value
+                if j == len(tiles) - 1:
+                    lower[sides[m], outs[n]] = lowers[m, n]
+
+            return run
+
+        count = len(tiles)
+        for m in range(len(sides)):
+            up(0, m)()
+        taken = 0
+        for j in range(count + 1):
+            units, pieces = [], []
+            if j >= 1:
+                units += [down(j - 1, m, n) for m in range(len(sides)) for n in range(len(outs))]
+            if j + 1 < count:
+                units += [up(j + 1, m) for m in range(len(sides))]
+            if j < count:
+                pieces += [act(j, m, k) for m in range(len(sides)) for k in range(side_tile // 64)]
+            upto = len(extra) * (j + 1) // (count + 1)
+            pieces += extra[taken:upto]
+            taken = upto
+            interleave(units, pieces)
+
+    def second_norm(r):
+        def piece():
+            w, at = r.start // rows_here, r.start % rows_here
+            window = pl.ds(at, fine)
+            keep = keeps[1, jnp.maximum(step - 1, 0) * group + w]
+            n2, s2 = normalize(lower[r, :] + down_b[...])
+            value = middle[r, :] + (n2 * gain2[...] + bias2[...])
+            out[w, window, :] = (value * keep).astype(jnp.bfloat16)
+            incoming = cot[w, window, :].astype(jnp.float32) * keep
+            low = normalize_back(incoming, n2, s2, gain2[...]).astype(jnp.bfloat16)
+            lower_out[r, :] = low
+            mid_grad[r, :] = incoming
+            add_vec(0, incoming * n2)
+            add_vec(1, incoming)
+            add_vec(2, low.astype(jnp.float32))
+
+        return piece
+
+    def backward_slots(extra):
+        hids, mids = {}, {}
+
+        def hid(j, m):
+            def run():
+                hids[j, m] = dot_nt(lower_out[sides[m], :], down_w[tiles[j], :])
+
+            return run
+
+        def act(j, m, k):
+            def run():
+                at = slice(k * 64, (k + 1) * 64)
+                r = slice(m * side_tile + k * 64, m * side_tile + (k + 1) * 64)
+                low = (hids[j, m][at] * slope[r, tiles[j]]).astype(jnp.bfloat16)
+                upper_out[r, tiles[j]] = low
+                upb_acc[:, tiles[j]] += rows_in_eights(low.astype(jnp.float32))
+
+            return run
+
+        def mid(j, m, n):
+            def run():
+                value = dot_nt(upper_out[sides[m], tiles[j]], up_w[outs[n], tiles[j]])
+                mids[m, n] = mids[m, n] + value if j > 0 else value
+                if j == len(tiles) - 1:
+                    mid_grad[sides[m], outs[n]] += mids[m, n]
+
+            return run
+
+        count = len(tiles)
+        for m in range(len(sides)):
+            hid(0, m)()
+        taken = 0
+        for j in range(count + 1):
+            units, pieces = [], []
+            if j >= 1:
+                units += [mid(j - 1, m, n) for m in range(len(sides)) for n in range(len(outs))]
+            if j + 1 < count:
+                units += [hid(j + 1, m) for m in range(len(sides))]
+            if j < count:
+                pieces += [act(j, m, k) for m in range(len(sides)) for k in range(side_tile // 64)]
+            upto = len(extra) * (j + 1) // (count + 1)
+            pieces += extra[taken:upto]
+            taken = upto
+            interleave(units, pieces)
+
+    def first_back(r):
+        def piece():
+            w, at = r.start // rows_here, r.start % rows_here
+            window = pl.ds(at, fine)
+            low = mid_grad[r, :].astype(jnp.bfloat16)
+            mid_out[w, window, :] = low
+            grad = low.astype(jnp.float32)
+            n1 = n1_all[back_slot, r, :]
+            add_vec(3, grad * n1)
+            add_vec(4, grad)
+            pre_low = normalize_back(grad, n1, q1_all[back_slot, r, :], gain1[...]).astype(jnp.bfloat16)
+            pre_keep[keep_slot, w, window, :] = pre_low
+            add_vec(5, pre_low.astype(jnp.float32))
+
+        return piece
 
     @pl.when(step == 0)
     def _():
@@ -226,99 +474,173 @@
             def _():
                 pl.semaphore_signal(barrier, inc=1, device_id=other[side], device_id_type=MESH)
 
+        vec_acc[...] = jnp.zeros_like(vec_acc)
+        upb_acc[...] = jnp.zeros_like(upb_acc)
+        mid_grad[...] = jnp.zeros_like(mid_grad)
+        n1_all[...] = jnp.zeros_like(n1_all)
+        q1_all[...] = jnp.zeros_like(q1_all)
         pl.semaphore_wait(barrier, (s > 0).astype(jnp.int32) + (s < last).astype(jnp.int32))
+        near_first(lambda side: halo(0, side, 0).start())
+        near_first(lambda side: halo(0, side, 1).start())
+        for i in range(1, AHEAD):
+            near_first(lambda side: halo(i, side).start())
         for side in range(2):
-
-            @pl.when(has[side])
-            def _():
-                halo(0, side).start()
 
             @pl.when(jnp.logical_not(has[side]))
             def _():
                 land = (from_l, from_r)[side]
                 land[...] = jnp.zeros_like(land)
 
+    @pl.when(step + AHEAD < blocks)
+    def _():
+        near_first(lambda side: halo(step + AHEAD, side).start())
+
     for side in range(2):
 
-        @pl.when(has[side])
+        @pl.when(has[side] & (step > 0) & (step < blocks))
         def _():
             halo_in(step, side).wait_recv()
 
-            @pl.when(step + 1 < steps)
-            def _():
-                halo(step + 1, side).start()
-
-    rows = pl.ds(step * group, group)
-    parts = (from_l.at[rows], x_mid, from_r.at[rows])
-    refs_in = inner[:11] + inner[11:15] + [d_ffn, d_vec, hidden, slope]
-    pre_low = block_compute(step, 1, keeps, parts, refs_in)
-    for side in range(2):
-
-        @pl.when(has[side] & (step >= 2))
+        @pl.when(has[side] & (step >= 4) & (step - 4 < EARLY))
         def _():
-            back(step - 2, side).wait_send()
-
-    pre_keep[lax.rem(step, 2)] = pre_low
-    for side in range(2):
-
-        @pl.when(has[side])
-        def _():
-            back(step, side).start()
-
-    @pl.when(step == steps - 1)
+            back(step - 4, side).wait_send()
+
+    puts(False, (0, step - 1), (1, step - 2), (2, step - 3), (3, step - 3))
+
+    @pl.when((step > 0) & (step < blocks))
     def _():
+        forward_slots([build_ext(w) for w in range(group)] + [first_back(r) for r in fine_rows])
+        puts(True, (0, step), (1, step - 1), (2, step - 2), (3, step - 2))
+        near_first(lambda side: pl.when((step >= 2) & (step - 2 < EARLY))(lambda: back(step - 2, side).start()))
+        puts(False, (4, step - 2), (5, step - 2))
+        interleave(conv_units(), [second_norm(r) for r in fine_rows])
+        puts(True, (4, step - 1), (5, step - 1))
+        puts(False, (6, step - 2), (7, step - 1))
+        backward_slots([first_norm(r) for r in fine_rows])
+        puts(True, (6, step - 1), (7, step))
+
+    @pl.when(step == 0)
+    def _():
+        units = conv_units()
+        for part in range(2):
+            for side in range(2):
+                pl.when(has[side])(lambda: halo_in(0, side, part).wait_recv())
+            for w in range(part * per_side, (part + 1) * per_side):
+                build_ext(w)()
+            half = len(units) // 2
+            pieces = [first_norm(r) for r in fine_rows[: len(fine_rows) // 2]] if part else []
+            interleave(units[part * half : (part + 1) * half], pieces)
+        for r in fine_rows[len(fine_rows) // 2 :]:
+            first_norm(r)()
+        puts(True, (0, step), (7, step))
+
+    @pl.when(step == blocks)
+    def _():
+        forward_slots([first_back(r) for r in fine_rows])
+        puts(True, (1, step - 1), (2, step - 2), (3, step - 2))
+        puts(False, (4, step - 2), (5, step - 2))
+        for r in fine_rows:
+            second_norm(r)()
+        puts(True, (4, step - 1), (5, step - 1))
+        puts(False, (6, step - 2), (7, step - 1))
+        backward_slots([])
+        puts(True, (6, step - 1))
+
+    @pl.when(step == blocks + 1)
+    def _():
+        for r in fine_rows:
+            first_back(r)()
+        puts(True, (2, step - 2), (3, step - 2))
+        puts(False, (4, step - 2), (5, step - 2), (6, step - 2))
+
+    @pl.when(step == blocks + 1)
+    def _():
+        for k in range(6):
+            d_vec[k : k + 1, :] = col_sum(vec_acc[k])
+        d_vec[6:8, :] = jnp.zeros((2, width), jnp.float32)
+        for k in range(ff // width):
+            d_vec[8 + k : 9 + k, :] = col_sum(upb_acc[:, k * width : (k + 1) * width])
+        for k in range(8 + ff // width, d_vec.shape[0]):
+            d_vec[k : k + 1, :] = jnp.zeros((1, width), jnp.float32)
+        put(2, blocks - 1).wait()
+        put(3, blocks - 1).wait()
         for side in range(2):
 
             @pl.when(has[side])
             def _():
-                for i in range(steps):
+                for part in range(2):
+                    halo(0, side, part).wait_send()
+                for i in range(1, blocks):
                     halo(i, side).wait_send()
+                for i in range(EARLY):
                     back_in(i, side).wait_recv()
-                for i in range(max(0, steps - 2), steps):
-                    back(i, side).wait_send()
 
 
 def block_params(conv_w, conv_b, gain1, bias1, up_w, up_b, down_w, down_b, gain2, bias2):
     row = lambda v: v.reshape(1, -1)
     return [conv_w, row(conv_b), row(gain1), row(bias1), up_w, row(up_b), down_w, row(down_b), row(gain2), row(bias2)]
+
+
+def flat_specs(rows, ff, width):
+    return [pl.BlockSpec((rows, w), lambda i: (i, 0)) for w in (ff, ff, width, width)]
+
+
+def flat_shapes(rows, ff, width):
+    return [jax.ShapeDtypeStruct((rows, w), jnp.bfloat16) for w in (ff, ff, width, width)]
 
 
 def blocks_halo(keeps, x, cot, params):
     windows, rows_here, width = cot.shape
     ff = params[4].shape[1]
     group = TILE_ROWS // rows_here
-    steps = windows // group
+    count = windows // group
     rows = group * rows_here
-    tile = pl.BlockSpec((group, rows_here, width), lambda i: (i, 0, 0))
-    wide = pl.BlockSpec((group, 3 * rows_here, width), lambda i: (i, 0, 0))
+
+    def late(by):
+        return lambda i: jnp.clip(i - by, 0, count - 1)
+
+    def tile(by):
+        return pl.BlockSpec((group, rows_here, width), lambda i: (late(by)(i), 0, 0))
+
     whole = pl.BlockSpec(memory_space=pltpu.VMEM)
     anywhere = pl.BlockSpec(memory_space=pl.ANY)
     like = jax.ShapeDtypeStruct(cot.shape, jnp.bfloat16)
+    square = pltpu.VMEM((rows, width), jnp.float32)
+    block = pltpu.VMEM((group, rows_here, width), jnp.bfloat16)
+    dma = pltpu.SemaphoreType.DMA((count + 1, 2))
     return pl.pallas_call(
-        functools.partial(block_halo_kernel, steps),
-        grid=(steps,),
-        in_specs=[pl.BlockSpec(memory_space=pltpu.SMEM), anywhere, tile, tile] + [whole] * len(params),
-        out_specs=[tile, wide, tile, tile, anywhere, anywhere, whole, whole],
-        out_shape=[
-            like,
-            jax.ShapeDtypeStruct((windows, 3 * rows_here, width), jnp.bfloat16),
-            like,
-            like,
-            like,
-            like,
-            jax.ShapeDtypeStruct((2 * ff // FF_TILE, width, FF_TILE), jnp.float32),
-            jax.ShapeDtypeStruct((16, width), jnp.float32),
-        ],
+        functools.partial(block_halo_kernel, count),
+        grid=(count + 2,),
+        in_specs=[pl.BlockSpec(memory_space=pltpu.SMEM), anywhere, tile(0), tile(1)] + [whole] * len(params),
+        out_specs=[anywhere] * 10 + [whole],
+        out_shape=[like, jax.ShapeDtypeStruct((windows, 3 * rows_here, width), jnp.bfloat16), like, like]
+        + flat_shapes(windows * rows_here, ff, width)
+        + [like, like, jax.ShapeDtypeStruct((16, width), jnp.float32)],
         scratch_shapes=[
+            block,
+            pltpu.VMEM((group, 3 * rows_here, width), jnp.bfloat16),
+            block,
             pltpu.VMEM((rows, ff), jnp.bfloat16),
+            pltpu.VMEM((rows, ff), jnp.bfloat16),
+            pltpu.VMEM((rows, width), jnp.bfloat16),
             pltpu.VMEM((rows, ff), jnp.float32),
+            square,
+            pltpu.VMEM((2, rows, width), jnp.float32),
+            pltpu.VMEM((2, rows, width), jnp.float32),
+            square,
+            pltpu.VMEM((rows, width), jnp.bfloat16),
+            square,
+            square,
+            pltpu.VMEM((6, 8, width), jnp.float32),
+            pltpu.VMEM((8, ff), jnp.float32),
             pltpu.VMEM(cot.shape, jnp.bfloat16),
             pltpu.VMEM(cot.shape, jnp.bfloat16),
             pltpu.VMEM((2, group, rows_here, width), jnp.bfloat16),
-            pltpu.SemaphoreType.DMA((steps, 2)),
-            pltpu.SemaphoreType.DMA((steps, 2)),
-            pltpu.SemaphoreType.DMA((steps, 2)),
-            pltpu.SemaphoreType.DMA((steps, 2)),
+            dma,
+            dma,
+            dma,
+            dma,
+            pltpu.SemaphoreType.DMA((8,)),
         ],
         compiler_params=pltpu.CompilerParams(
             vmem_limit_bytes=VMEM_BYTES, collective_id=0, has_side_effects=True
@@ -341,16 +663,11 @@
         functools.partial(block_kernel, depth),
         grid=(windows // group,),
         in_specs=[pl.BlockSpec(memory_space=pltpu.SMEM)] + [tile] * (len(parts) + 1) + [whole] * len(params),
-        out_specs=[tile, wide, tile, tile, whole, whole],
-        out_shape=[
-            like,
-            jax.ShapeDtypeStruct((windows, (2 * depth + 1) * rows_here, width), jnp.bfloat16),
-            like,
-            like,
-            jax.ShapeDtypeStruct((2 * ff // FF_TILE, width, FF_TILE), jnp.float32),
-            jax.ShapeDtypeStruct((16, width), jnp.float32),
-        ],
-        scratch_shapes=[pltpu.VMEM((rows, ff), jnp.bfloat16), pltpu.VMEM((rows, ff), jnp.float32)],
+        out_specs=[tile, wide, tile, tile] + flat_specs(rows, ff, width) + [whole],
+        out_shape=[like, jax.ShapeDtypeStruct((windows, (2 * depth + 1) * rows_here, width), jnp.bfloat16), like, like]
+        + flat_shapes(windows * rows_here, ff, width)
+        + [jax.ShapeDtypeStruct((16, width), jnp.float32)],
+        scratch_shapes=[pltpu.VMEM((rows, ff), jnp.float32)],
         compiler_params=pltpu.CompilerParams(vmem_limit_bytes=VMEM_BYTES),
         name="block_general",
     )(keeps, *parts, cot, *params)
@@ -411,6 +728,7 @@
 
 class Reducer:
     stages = 8
+    gap = 2
 
     def __init__(self, count, acc, res, res_out, bufs, sems):
         self.count, self.acc, self.res, self.res_out = count, acc, res, res_out
@@ -597,7 +915,7 @@
 
     def tick(self, t):
         for stage in range(self.stages, -1, -1):
-            c = t - stage
+            c = t - stage * self.gap
 
             @pl.when((c >= 0) & (c < self.count))
             def _():
@@ -608,16 +926,21 @@
             self.write_out(jnp.int32(c), lambda copy: copy.wait())
 
 
+def hidden_width(tiles):
+    return tiles.shape[2]
+
+
 def reduce_kernel(steps, *refs):
     (
-        keeps, ffn, vec_in, ext_hbm, pre_hbm, pre_l, pre_r, mid_hbm, conv_w,
-        grad_out, up_out, down_out, conv_out, vec_out,
-        ext, pre, acc, res, pext, midb, gout, vsend, vrecv,
-    ) = refs[:23]
-    bufs = refs[23:34]
-    sems = refs[34:51]
-    load_s, ffn_s, in_s, gout_s, v_s, v_r = refs[51:]
-    ffn_count = ffn.shape[0]
+        keeps, hidden, upper, lower_hbm, middle_hbm, vec_in, ext_hbm, pre_hbm, pre_l, pre_r, mid_hbm, conv_w,
+        grad_out, up_out, down_out, conv_out, vec_out, late_l, late_r,
+        ext, pre, lower, middle, tiles, acc, res, pext, midb, gout, vsend, vrecv,
+    ) = refs[:31]
+    bufs = refs[31:42]
+    sems = refs[42:59]
+    load_s, ffn_s, in_s, gout_s, v_s, v_r, late_s, late_q = refs[59:]
+    ff_tiles = hidden.shape[1] // hidden_width(tiles)
+    ffn_count = 2 * ff_tiles
     count = ffn_count + KERNEL
     group, rows_here, width = gout.shape[1:]
     rows = group * rows_here
@@ -625,42 +948,112 @@
     s = lax.axis_index("seq")
     last = lax.axis_size("seq") - 1
 
+    b = lax.axis_index("batch")
+    has = (s > 0, s < last)
+    other = ((s - 1, b), (s + 1, b))
+    beyond = jnp.where(red.core == 0, s - 1, s + 1)
+    has_beyond = (beyond >= 0) & (beyond <= last)
+
     barrier = pltpu.get_barrier_semaphore()
     for peer in red.peers():
         pl.semaphore_signal(barrier, inc=1, device_id=peer, device_id_type=MESH)
 
+    @pl.when(has_beyond)
+    def _():
+        pl.semaphore_signal(barrier, inc=1, device_id=(beyond, b), device_id_type=MESH)
+
+    def late(i, side):
+        at = pl.ds((i - EARLY) * group, group)
+        land = (late_r, late_l)[side]
+        k = i - EARLY
+        return remote(
+            pre_hbm.at[pl.ds(i * group, group)], land.at[at], late_s.at[k, side], late_q.at[k, side], other[side]
+        )
+
+    def late_in(i, side):
+        at = pl.ds((i - EARLY) * group, group)
+        land = (late_l, late_r)[side]
+        k = i - EARLY
+        return remote(
+            pre_hbm.at[pl.ds(i * group, group)], land.at[at], late_s.at[k, side], late_q.at[k, 1 - side], other[side]
+        )
+
     load_ext = pltpu.make_async_copy(ext_hbm, ext, load_s.at[0])
     load_pre = pltpu.make_async_copy(pre_hbm, pre, load_s.at[1])
 
-    def load_ffn(c):
+    load_lower = pltpu.make_async_copy(lower_hbm, lower, load_s.at[2])
+    load_middle = pltpu.make_async_copy(middle_hbm, middle, load_s.at[3])
+    tile_rows = tiles.shape[1]
+    per_chunk = lower.shape[0] // tile_rows
+
+    def load_tile(i, act):
+        r = lax.rem(i, 2)
+        c = lax.div(i, per_chunk)
+        at = pl.ds(pl.multiple_of(lax.rem(i, per_chunk) * tile_rows, tile_rows), tile_rows)
+
+        def copy(source, first):
+            cols = pl.ds(pl.multiple_of((c - first) * width, width), width)
+            return lambda: act(pltpu.make_async_copy(source.at[at, cols], tiles.at[r], ffn_s.at[r]))
+
+        pl.when(c < ff_tiles)(copy(upper, 0))
+        pl.when((c >= ff_tiles) & (c < ffn_count))(copy(hidden, ff_tiles))
+
+    def ffn_grad(c):
         r = lax.rem(c, RING)
-        return pltpu.make_async_copy(ffn.at[c], acc.at[r], ffn_s.at[r])
-
-    def load_rows(i):
+
+        def part(i):
+            tile = c * per_chunk + i
+            load_tile(tile, lambda copy: copy.wait())
+            load_tile(tile + 1, lambda copy: copy.start())
+            at = pl.ds(pl.multiple_of(i * tile_rows, tile_rows), tile_rows)
+            slot = lax.rem(tile, 2)
+
+            def add(value):
+                @pl.when(i == 0)
+                def _():
+                    acc[r] = value
+
+                @pl.when(i > 0)
+                def _():
+                    acc[r] += value
+
+            pl.when(c < ff_tiles)(lambda: add(dot_tn(middle[at], tiles[slot])))
+            pl.when(c >= ff_tiles)(lambda: add(dot_tn(tiles[slot], lower[at])))
+
+        lax.fori_loop(0, per_chunk, lambda i, _: (part(i), 0)[1], 0)
+
+    def each_load(i, act, fresh=False):
         slot = lax.rem(i, 2)
         at = pl.ds(i * group, group)
-        return (
-            pltpu.make_async_copy(pre_l.at[at], pext.at[slot, :, pl.ds(0, rows_here)], in_s.at[slot, 0]),
-            pltpu.make_async_copy(pre_hbm.at[at], pext.at[slot, :, pl.ds(rows_here, rows_here)], in_s.at[slot, 1]),
-            pltpu.make_async_copy(pre_r.at[at], pext.at[slot, :, pl.ds(2 * rows_here, rows_here)], in_s.at[slot, 2]),
-            pltpu.make_async_copy(mid_hbm.at[at], midb.at[slot], in_s.at[slot, 3]),
-        )
-
-    def each_load(i, act):
-        a, m, z, d = load_rows(i)
-        pl.when(s > 0)(lambda: act(a))
-        act(m)
-        pl.when(s < last)(lambda: act(z))
-        act(d)
+        at_late = pl.ds((i - EARLY) * group, group)
+        for side, early_ref, late_ref in ((0, pre_l, late_l), (1, pre_r, late_r)):
+            to = pext.at[slot, :, pl.ds(2 * side * rows_here, rows_here)]
+            sem = in_s.at[slot, side]
+
+            @pl.when(has[side] & (i < EARLY))
+            def _():
+                act(pltpu.make_async_copy(early_ref.at[at], to, sem))
+
+            @pl.when(has[side] & (i >= EARLY))
+            def _():
+                if fresh:
+                    late_in(i, side).wait_recv()
+                act(pltpu.make_async_copy(late_ref.at[at_late], to, sem))
+
+        act(pltpu.make_async_copy(pre_hbm.at[at], pext.at[slot, :, pl.ds(rows_here, rows_here)], in_s.at[slot, 2]))
+        act(pltpu.make_async_copy(mid_hbm.at[at], midb.at[slot], in_s.at[slot, 3]))
 
     def store_rows(i):
         slot = lax.rem(i, 2)
         return pltpu.make_async_copy(gout.at[slot], grad_out.at[pl.ds(i * group, group)], gout_s.at[slot])
 
-    load_ffn(0).start()
-    each_load(0, lambda copy: copy.start())
+    load_middle.start()
+    for i in range(1):
+        load_tile(jnp.int32(i), lambda copy: copy.start())
+    load_lower.start()
     load_ext.start()
     load_pre.start()
+    each_load(0, lambda copy: copy.start())
     for side, at in ((s > 0, 0), (s < last, 2)):
 
         @pl.when(jnp.logical_not(side))
@@ -669,7 +1062,10 @@
                 (2, group, rows_here, width), jnp.bfloat16
             )
 
-    pl.semaphore_wait(barrier, len(red.peers()))
+    pl.semaphore_wait(barrier, len(red.peers()) + has_beyond.astype(jnp.int32))
+    for i in range(EARLY, steps):
+        for side in range(2):
+            pl.when(has[side])(lambda: late(i, side).start())
 
     def vec_copy(q):
         return remote(vsend.at[q], vrecv.at[q], v_s.at[q], v_r.at[q], red.vec_peers[q])
@@ -679,7 +1075,7 @@
 
         @pl.when(i + 1 < steps)
         def _():
-            each_load(i + 1, lambda copy: copy.start())
+            each_load(i + 1, lambda copy: copy.start(), True)
 
         slot = lax.rem(i, 2)
         grad = jnp.zeros((rows, width), jnp.float32)
@@ -702,21 +1098,12 @@
         r = lax.rem(ffn_count + tap, RING)
         begin = pl.multiple_of(tap * DILATION, DILATION)
 
-        def part(i, first):
-            at = pl.ds(i * 2 * group, 2 * group)
-            taken = ext[at, pl.ds(begin, rows_here), :].reshape(2 * rows, width)
-            grads = pre[at].reshape(2 * rows, width)
-            value = dot_tn(taken, grads)
-            acc[r] = value if first else acc[r] + value
-
-        part(0, True)
-        lax.fori_loop(1, steps // 2, lambda i, _: (part(i, False), 0)[1], 0)
+        taken = ext[:, pl.ds(begin, rows_here), :].reshape(steps * rows, width)
+        acc[r] = dot_tn(taken, pre[...].reshape(steps * rows, width))
+
+    load_middle.wait()
 
     def tick(t, _):
-        @pl.when(t < ffn_count)
-        def _():
-            load_ffn(t).wait()
-
         red.tick(t)
         for q in range(6):
 
@@ -733,20 +1120,28 @@
                 else:
                     vec_out[...] = value
 
-        @pl.when(t + 1 < ffn_count)
+        chunk = t + 1
+
+        @pl.when(chunk == ff_tiles)
         def _():
-            load_ffn(t + 1).start()
-
-        @pl.when(t < steps)
+            load_lower.wait()
+
+        @pl.when(chunk < ffn_count)
         def _():
-            row_block(t)
-
-        @pl.when(t == ffn_count - 1)
+            ffn_grad(chunk)
+
+        @pl.when(chunk == ffn_count)
         def _():
             load_ext.wait()
             load_pre.wait()
 
-        tap = t + 1 - ffn_count
+        rest = t - (count - 1)
+
+        @pl.when((rest >= 0) & (rest < steps))
+        def _():
+            row_block(rest)
+
+        tap = chunk - ffn_count
 
         @pl.when((tap >= 0) & (tap < KERNEL))
         def _():
@@ -754,35 +1149,44 @@
 
         return 0
 
-    lax.fori_loop(0, count + red.stages, tick, 0)
+    lax.fori_loop(-1, count + red.stages * red.gap, tick, 0)
     red.finish()
+    for i in range(EARLY, steps):
+        for side in range(2):
+            pl.when(has[side])(lambda: late(i, side).wait_send())
     for i in range(max(0, steps - 2), steps):
         store_rows(i).wait()
 
 
-def reduce_all(keeps, ffn, vec, ext, pre, pre_l, pre_r, mid, conv_w):
+def reduce_all(keeps, hidden, upper, lower, middle, vec, ext, pre, pre_l, pre_r, mid, conv_w):
     windows, rows_here, width = pre.shape
+    ff = hidden.shape[1]
     group = TILE_ROWS // rows_here
     steps = windows // group
-    count = ffn.shape[0] + KERNEL
+    count = 2 * ff // width + KERNEL
     whole = pl.BlockSpec(memory_space=pltpu.VMEM)
     anywhere = pl.BlockSpec(memory_space=pl.ANY)
     dma = pltpu.SemaphoreType.DMA
     half = width // 2
+    rows = group * rows_here
     return pl.pallas_call(
         functools.partial(reduce_kernel, steps),
-        in_specs=[pl.BlockSpec(memory_space=pltpu.SMEM), anywhere, whole] + [anywhere] * 5 + [whole],
-        out_specs=[anywhere] * 4 + [whole],
+        in_specs=[pl.BlockSpec(memory_space=pltpu.SMEM), anywhere, anywhere, anywhere, anywhere, whole] + [anywhere] * 5 + [whole],
+        out_specs=[anywhere] * 4 + [whole, anywhere, anywhere],
         out_shape=[
             jax.ShapeDtypeStruct(pre.shape, jnp.bfloat16),
-            jax.ShapeDtypeStruct((width, ffn.shape[0] // 2 * width), jnp.bfloat16),
-            jax.ShapeDtypeStruct((ffn.shape[0] // 2 * width, width), jnp.bfloat16),
+            jax.ShapeDtypeStruct((width, ff), jnp.bfloat16),
+            jax.ShapeDtypeStruct((ff, width), jnp.bfloat16),
             jax.ShapeDtypeStruct((KERNEL, width, width), jnp.bfloat16),
             jax.ShapeDtypeStruct(vec.shape, jnp.float32),
-        ],
+        ]
+        + [jax.ShapeDtypeStruct(((steps - EARLY) * group, rows_here, width), jnp.bfloat16)] * 2,
         scratch_shapes=[
             pltpu.VMEM(ext.shape, jnp.bfloat16),
             pltpu.VMEM(pre.shape, jnp.bfloat16),
+            pltpu.VMEM(lower.shape, jnp.bfloat16),
+            pltpu.VMEM(middle.shape, jnp.bfloat16),
+            pltpu.VMEM((2, 4 * rows, width), jnp.bfloat16),
             pltpu.VMEM((RING, width, width), jnp.float32),
             pltpu.VMEM((count, width, width), jnp.bfloat16),
             pltpu.VMEM((2, group, 3 * rows_here, width), jnp.bfloat16),
@@ -807,12 +1211,13 @@
             dma((RING, 3)), dma((RING, 3)), dma((RING, 3, 2)), dma((RING, 3, 2)), dma((RING, 2)), dma((RING, 2)),
             dma((RING, 2)), dma((RING, 2)), dma((RING,)), dma((RING,)), dma((2,)),
         ]
-        + [dma((2,)), dma((RING,)), dma((2, 4)), dma((2,)), dma((5,)), dma((5,))],
+        + [dma((4,)), dma((RING,)), dma((2, 4)), dma((2,)), dma((5,)), dma((5,))]
+        + [dma((steps - EARLY, 2)), dma((steps - EARLY, 2))],
         compiler_params=pltpu.CompilerParams(
             vmem_limit_bytes=VMEM_BYTES, collective_id=1, has_side_effects=True
         ),
         name="reduce",
-    )(keeps, ffn, vec, ext, pre, pre_l, pre_r, mid, conv_w)
+    )(keeps, hidden, upper, lower, middle, vec, ext, pre, pre_l, pre_r, mid, conv_w)
 
 
 def spread(shard, depth):
@@ -847,18 +1252,19 @@
     )
     tiles = ff // FF_TILE
     if (lax.axis_size("seq"), lax.axis_size("batch"), rows_here) == (8, 4, REACH):
-        out, ext, pre_low, mid_low, pre_l, pre_r, d_ffn, d_vec = blocks_halo(keeps, block_input, out_cotangent, params)
-        input_grad, d_up, d_down, d_conv, d_vec = reduce_all(
-            keeps, d_ffn, d_vec, ext, pre_low, pre_l, pre_r, mid_low, conv_weight
+        out, ext, pre_low, mid_low, hidden, upper, lower, middle, pre_l, pre_r, d_vec = blocks_halo(
+            keeps, block_input, out_cotangent, params
+        )
+        input_grad, d_up, d_down, d_conv, d_vec, _, _ = reduce_all(
+            keeps, hidden, upper, lower, middle, d_vec, ext, pre_low, pre_l, pre_r, mid_low, conv_weight
         )
         d_up, d_down, d_conv = (d.astype(jnp.float32) for d in (d_up, d_down, d_conv))
     else:
         parts = spread(block_input, depth)
-        out, _, pre_low, mid_low, d_ffn, d_vec = blocks(keeps, parts, out_cotangent, params)
+        out, _, pre_low, mid_low, hidden, upper, lower, middle, d_vec = blocks(keeps, parts, out_cotangent, params)
         input_grad, d_conv = conv_back(keeps, spread(pre_low, depth), block_input, mid_low, conv_weight)
-        d_ffn, d_conv, d_vec = lax.psum((d_ffn, d_conv, d_vec), ("seq", "batch"))
-        d_up = d_ffn[:tiles].transpose(1, 0, 2).reshape(width, ff)
-        d_down = d_ffn[tiles:].reshape(ff, width)
+        d_up, d_down = dot_tn(middle, upper), dot_tn(hidden, lower)
+        d_up, d_down, d_conv, d_vec = lax.psum((d_up, d_down, d_conv, d_vec), ("seq", "batch"))
     return (
         out,
         input_grad,

time: 269 us -> 243 us (0.903)
  Pallas kernels: 244 us -> 219 us
    pallas_call x1, Pallas kernels: 119 us -> 96.1 us  [blocks_halo(): pl.pallas_call(functools.partial(block_halo_kernel, count), grid=(count +...]
where the time goes in v3:
time: 243 us
  Pallas kernels  219 us (90%)
  other arithmetic  13.3 us (5%)
  local copies, waits for them, and re-layouts  9.85 us (4%)
    pallas_call x1, Pallas kernels, reduce_all(): pl.pallas_call(functools.partial(reduce_kernel, steps), in_specs=[pl.Bloc...  123 us
    pallas_call x1, Pallas kernels, blocks_halo(): pl.pallas_call(functools.partial(block_halo_kernel, count), grid=(count +...  96.1 us
    convert_element_type x3, other arithmetic, per_device(): d.astype(jnp.float32)  12 us
    unnamed x12, local copies, waits for them, and re-layouts  8.31 us

profile of v3, /device:TPU:0, one launch (start us, length us, event | category | flops | bytes accessed | tf_op | source)
XLA Modules:
  0.0 242.7 jit_solution(9997963700080447966)
XLA Ops:
  0.7 1.3 compare_convert_fusion.refs_0_
  2.0 96.1 %block.1 = (bf16[32,128,512]{2,1,0:T(8,128)(2,1)}, bf16[32,384,512]{2,1,0:T(8,128)(2,1)}, bf16[32,128,512]{2,1,0:T(8,128)(2,1)}, bf16[32,128,512]{2,1,0:T(8,128)...) custom-call(f32[3,32]{1,0:T(4,128)} %compare_convert_fusion.refs_0_,, ...), custom_call_target="tpu_custom_call" | custom-call | tf_op jit(solution)/shard_map/block/pallas_call | solution.py:611
  98.1 122.8 %reduce.1 = (bf16[32,128,512]{2,1,0:T(8,128)(2,1)}, bf16[512,2048]{1,0:T(8,128)(2,1)}, bf16[2048,512]{1,0:T(8,128)(2,1)}, bf16[9,512,512]{2,1,0:T(8,128)(2,1)}, ...) custom-call(f32[3,32]{1,0:T(4,128)} %compare_convert_fusion.refs_0_, ...), custom_call_target="tpu_custom_call" | custom-call | tf_op jit(solution)/shard_map/reduce/pallas_call | solution.py:1172
  220.8 0.0 copy-start.3
  220.9 0.9 slice_bitcast_fusion
  221.7 1.5 fusion
  223.3 0.6 copy.25
  223.9 4.1 %convert_element_type.14 = f32[512,2048]{1,0:T(8,128)} convert(bf16[512,2048]{1,0:T(8,128)(2,1)} %get-tuple-element.42) | non-fusion elementwise | flops 1048576 | bytes 6291456 | tf_op jit(solution)/shard_map/convert_element_type | solution.py:1261
  228.0 0.0 copy-done.3
  228.0 0.0 copy-start
  228.0 2.7 %convert_element_type.15 = f32[2048,512]{1,0:T(8,128)} convert(bf16[2048,512]{1,0:T(8,128)(2,1)S(1)} %copy-done.3) | non-fusion elementwise | flops 1048576 | bytes 6291456 | tf_op jit(solution)/shard_map/convert_element_type | solution.py:1261
  230.7 1.1 copy-done
  231.9 0.0 copy-start.1
  231.9 5.1 %convert_element_type.13 = f32[9,512,512]{2,1,0:T(8,128)} convert(bf16[9,512,512]{2,1,0:T(8,128)(2,1)S(1)} %copy-done) | non-fusion elementwise | flops 2359296 | bytes 14155776 | tf_op jit(solution)/shard_map/convert_element_type | solution.py:1261
  237.0 0.0 copy-done.1
  237.0 0.0 copy-start.2
  237.0 2.1 copy.28
  239.1 1.6 copy-done.2
  240.7 2.0 copy.29
  (1 shorter events, 0.0 us)
Async XLA Ops:
  220.8 7.2 %copy-start.3 = (bf16[2048,512]{1,0:T(8,128)(2,1)S(1)}, bf16[2048,512]{1,0:T(8,128)(2,1)}, u32[]{:S(2)}) copy-start(bf16[2048,512]{1,0:T(8,128)(2,1)} %get-tuple-element.43) | copy-start | bytes 6291460
  228.0 3.9 %copy-start = (bf16[9,512,512]{2,1,0:T(8,128)(2,1)S(1)}, bf16[9,512,512]{2,1,0:T(8,128)(2,1)}, u32[]{:S(2)}) copy-start(bf16[9,512,512]{2,1,0:T(8,128)(2,1)} %get-tuple-element.40) | copy-start | bytes 14155780
  231.9 5.1 %copy-start.1 = (bf16[32,128,512]{2,1,0:T(8,128)(2,1)S(1)}, bf16[32,128,512]{2,1,0:T(8,128)(2,1)}, u32[]{:S(2)}) copy-start(bf16[32,128,512]{2,1,0:T(8,128)(2,1)} %get-tuple-element.62) | copy-start | bytes 12582916
  237.0 3.7 %copy-start.2 = (bf16[32,128,512]{2,1,0:T(8,128)(2,1)S(1)}, bf16[32,128,512]{2,1,0:T(8,128)(2,1)}, u32[]{:S(2)}) copy-start(bf16[32,128,512]{2,1,0:T(8,128)(2,1)} %get-tuple-element.63) | copy-start | bytes 12582916

commit v4 on v3

--- a/solution.py
+++ b/solution.py
@@ -1050,10 +1050,6 @@
     load_middle.start()
     for i in range(1):
         load_tile(jnp.int32(i), lambda copy: copy.start())
-    load_lower.start()
-    load_ext.start()
-    load_pre.start()
-    each_load(0, lambda copy: copy.start())
     for side, at in ((s > 0, 0), (s < last, 2)):
 
         @pl.when(jnp.logical_not(side))
@@ -1065,7 +1061,8 @@
     pl.semaphore_wait(barrier, len(red.peers()) + has_beyond.astype(jnp.int32))
     for i in range(EARLY, steps):
         for side in range(2):
-            pl.when(has[side])(lambda: late(i, side).start())
+            pl.when(has[1 - side] & (red.core == 0))(lambda: late(i, 1 - side).start())
+            pl.when(has[side] & (red.core == 1))(lambda: late(i, side).start())
 
     def vec_copy(q):
         return remote(vsend.at[q], vrecv.at[q], v_s.at[q], v_r.at[q], red.vec_peers[q])
@@ -1120,6 +1117,10 @@
                 else:
                     vec_out[...] = value
 
+        pl.when(t == 0)(lambda: load_lower.start())
+        pl.when(t == 2)(lambda: load_pre.start())
+        pl.when(t == 3)(lambda: load_ext.start())
+        pl.when(t == ffn_count)(lambda: each_load(0, lambda copy: copy.start()))
         chunk = t + 1
 
         @pl.when(chunk == ff_tiles)
@@ -1220,6 +1221,32 @@
     )(keeps, hidden, upper, lower, middle, vec, ext, pre, pre_l, pre_r, mid, conv_w)
 
 
+def widen_kernel(*refs):
+    for source, target in zip(refs[:3], refs[3:]):
+        target[...] = source[...].astype(jnp.float32)
+
+
+def widened(d_up, d_down, d_conv):
+    taps, width, _ = d_conv.shape
+    ff = d_down.shape[0]
+    parts = taps - 1
+    at = lambda i: (jnp.minimum(i, parts - 1), 0)
+    specs = [
+        pl.BlockSpec((width // parts, ff), at),
+        pl.BlockSpec((ff // parts, width), at),
+        pl.BlockSpec((1, width, width), lambda i: (i, 0, 0)),
+    ]
+    return pl.pallas_call(
+        widen_kernel,
+        grid=(taps,),
+        in_specs=specs,
+        out_specs=specs,
+        out_shape=[jax.ShapeDtypeStruct(d.shape, jnp.float32) for d in (d_up, d_down, d_conv)],
+        compiler_params=pltpu.CompilerParams(vmem_limit_bytes=VMEM_BYTES),
+        name="tail",
+    )(d_up, d_down, d_conv)
+
+
 def spread(shard, depth):
     return [
         shard if offset == 0 else passed_along(shard, "seq", offset)
@@ -1258,7 +1285,7 @@
         input_grad, d_up, d_down, d_conv, d_vec, _, _ = reduce_all(
             keeps, hidden, upper, lower, middle, d_vec, ext, pre_low, pre_l, pre_r, mid_low, conv_weight
         )
-        d_up, d_down, d_conv = (d.astype(jnp.float32) for d in (d_up, d_down, d_conv))
+        d_up, d_down, d_conv = widened(d_up, d_down, d_conv)
     else:
         parts = spread(block_input, depth)
         out, _, pre_low, mid_low, hidden, upper, lower, middle, d_vec = blocks(keeps, parts, out_cotangent, params)

time: 243 us -> 242 us (level)
  other arithmetic: 13.3 us -> 1.31 us
  Pallas kernels: 219 us -> 230 us
    convert_element_type x3 -> x0, other arithmetic: 12 us -> none  [per_device(): d.astype(jnp.float32)]
    pallas_call x0 -> x1, Pallas kernels: none -> 10.8 us  [widened(): pl.pallas_call(widen_kernel, grid=(taps,), in_specs=specs, out_specs=spec...]
    unnamed x12 -> x6, local copies, waits for them, and re-layouts: 8.31 us -> 8.13 us
where the time goes in v4:
time: 242 us; the launch traced here: 241 us
  Pallas kernels  230 us (95%)
  local copies, waits for them, and re-layouts  9.66 us (4%)
    pallas_call x1, Pallas kernels, reduce_all(): pl.pallas_call(functools.partial(reduce_kernel, steps), in_specs=[pl.Bloc...  123 us
    pallas_call x1, Pallas kernels, blocks_halo(): pl.pallas_call(functools.partial(block_halo_kernel, count), grid=(count +...  96.1 us
    pallas_call x1, Pallas kernels, widened(): pl.pallas_call(widen_kernel, grid=(taps,), in_specs=specs, out_specs=spec...  10.8 us
    unnamed x6, local copies, waits for them, and re-layouts  8.13 us

profile of v4, /device:TPU:0, one launch (start us, length us, event | category | flops | bytes accessed | tf_op | source)
XLA Modules:
  0.0 241.5 jit_solution(13762012947250946124)
XLA Ops:
  0.7 1.3 compare_convert_fusion.refs_0_
  2.0 96.1 %block.1 = (bf16[32,128,512]{2,1,0:T(8,128)(2,1)}, bf16[32,384,512]{2,1,0:T(8,128)(2,1)}, bf16[32,128,512]{2,1,0:T(8,128)(2,1)}, bf16[32,128,512]{2,1,0:T(8,128)...) custom-call(f32[3,32]{1,0:T(4,128)} %compare_convert_fusion.refs_0_,, ...), custom_call_target="tpu_custom_call" | custom-call | tf_op jit(solution)/shard_map/block/pallas_call | solution.py:611
  98.1 122.9 %reduce.1 = (bf16[32,128,512]{2,1,0:T(8,128)(2,1)}, bf16[512,2048]{1,0:T(8,128)(2,1)}, bf16[2048,512]{1,0:T(8,128)(2,1)}, bf16[9,512,512]{2,1,0:T(8,128)(2,1)}, ...) custom-call(f32[3,32]{1,0:T(4,128)} %compare_convert_fusion.refs_0_, ...), custom_call_target="tpu_custom_call" | custom-call | tf_op jit(solution)/shard_map/reduce/pallas_call | solution.py:1173
  221.0 0.7 slice_bitcast_fusion
  221.7 1.5 fusion
  223.2 0.6 copy.25
  223.8 10.8 %tail.1 = (f32[512,2048]{1,0:T(8,128)}, f32[2048,512]{1,0:T(8,128)}, f32[9,512,512]{2,1,0:T(8,128)}) custom-call(bf16[512,2048]{1,0:T(8,128)(2,1)} %get-tuple-element.43.refs_0_, bf16[2048,512]{1,0:T(8,128)(2,1)} %get-tuple-element.44.refs_1_, bf16[9,512,512]{2,1,0:T(8,128)(2,1)} %get-tuple-element.45.refs_2_), custom_call_target="tpu_custom_call" | custom-call | tf_op jit(solution)/shard_map/tail/pallas_call | solution.py:1239
  234.7 0.0 copy-start
  234.7 4.8 %copy.28 = bf16[32,128,512]{2,1,0:T(8,128)(2,1)} copy(bf16[32,128,512]{2,1,0:T(8,128)(2,1)} %get-tuple-element.68) | data formatting | bytes 8388608
  239.5 0.0 copy-done
  239.5 2.0 copy.29
  (1 shorter events, 0.0 us)
Async XLA Ops:
  234.7 4.8 %copy-start = (bf16[32,128,512]{2,1,0:T(8,128)(2,1)S(1)}, bf16[32,128,512]{2,1,0:T(8,128)(2,1)}, u32[]{:S(2)}) copy-start(bf16[32,128,512]{2,1,0:T(8,128)(2,1)} %get-tuple-element.69) | copy-start | bytes 12582916

commit v5 on v4

--- a/solution.py
+++ b/solution.py
@@ -208,12 +208,16 @@
 
 def block_halo_kernel(blocks, *refs):
     (
-        keeps, x_hbm, x_mid, cot, conv_w, conv_b, gain1, bias1, up_w, up_b, down_w, down_b, gain2, bias2,
+        keeps, x_hbm, x_mid, cot, conv_hbm, conv_b, gain1, bias1, up_hbm, up_b, down_hbm, down_b, gain2, bias2,
         out_hbm, ext_hbm, pre_hbm, mid_hbm, hidden_hbm, upper_hbm, lower_hbm, middle_hbm, pre_l, pre_r, d_vec,
         out, ext, mid_out, hidden, upper_out, lower_out,
         slope, conv_acc, n1_all, q1_all, middle, middle_low, lower, mid_grad, vec_acc, upb_acc,
-        from_l, from_r, pre_keep, fs, fr, bs, br, ps,
+        from_l, from_r, pre_keep, fs, fr, bs, br, ps, conv_w, up_w, down_w, ws,
     ) = refs
+    weight_loads = [
+        pltpu.make_async_copy(source, target, ws.at[k])
+        for k, (source, target) in enumerate(((conv_hbm, conv_w), (up_hbm, up_w), (down_hbm, down_w)))
+    ]
     group, rows_here, width = cot.shape
     rows = group * rows_here
     ff = up_w.shape[1]
@@ -481,6 +485,8 @@
         q1_all[...] = jnp.zeros_like(q1_all)
         pl.semaphore_wait(barrier, (s > 0).astype(jnp.int32) + (s < last).astype(jnp.int32))
         near_first(lambda side: halo(0, side, 0).start())
+        for load in weight_loads:
+            load.start()
         near_first(lambda side: halo(0, side, 1).start())
         for i in range(1, AHEAD):
             near_first(lambda side: halo(i, side).start())
@@ -521,6 +527,7 @@
 
     @pl.when(step == 0)
     def _():
+        weight_loads[0].wait()
         units = conv_units()
         for part in range(2):
             for side in range(2):
@@ -533,6 +540,8 @@
         for r in fine_rows[len(fine_rows) // 2 :]:
             first_norm(r)()
         puts(True, (0, step), (7, step))
+        for load in weight_loads[1:]:
+            load.wait()
 
     @pl.when(step == blocks)
     def _():
@@ -611,7 +620,8 @@
     return pl.pallas_call(
         functools.partial(block_halo_kernel, count),
         grid=(count + 2,),
-        in_specs=[pl.BlockSpec(memory_space=pltpu.SMEM), anywhere, tile(0), tile(1)] + [whole] * len(params),
+        in_specs=[pl.BlockSpec(memory_space=pltpu.SMEM), anywhere, tile(0), tile(1)]
+        + [anywhere if p.shape[0] > 1 else whole for p in params],
         out_specs=[anywhere] * 10 + [whole],
         out_shape=[like, jax.ShapeDtypeStruct((windows, 3 * rows_here, width), jnp.bfloat16), like, like]
         + flat_shapes(windows * rows_here, ff, width)
@@ -641,7 +651,9 @@
             dma,
             dma,
             pltpu.SemaphoreType.DMA((8,)),
-        ],
+        ]
+        + [pltpu.VMEM(p.shape, jnp.bfloat16) for p in params if p.shape[0] > 1]
+        + [pltpu.SemaphoreType.DMA((3,))],
         compiler_params=pltpu.CompilerParams(
             vmem_limit_bytes=VMEM_BYTES, collective_id=0, has_side_effects=True
         ),
@@ -932,13 +944,14 @@
 
 def reduce_kernel(steps, *refs):
     (
-        keeps, hidden, upper, lower_hbm, middle_hbm, vec_in, ext_hbm, pre_hbm, pre_l, pre_r, mid_hbm, conv_w,
+        keeps, hidden, upper, lower_hbm, middle_hbm, vec_in, ext_hbm, pre_hbm, pre_l, pre_r, mid_hbm, conv_hbm,
         grad_out, up_out, down_out, conv_out, vec_out, late_l, late_r,
         ext, pre, lower, middle, tiles, acc, res, pext, midb, gout, vsend, vrecv,
     ) = refs[:31]
     bufs = refs[31:42]
     sems = refs[42:59]
-    load_s, ffn_s, in_s, gout_s, v_s, v_r, late_s, late_q = refs[59:]
+    load_s, ffn_s, in_s, gout_s, v_s, v_r, late_s, late_q, conv_w = refs[59:]
+    load_conv = pltpu.make_async_copy(conv_hbm, conv_w, load_s.at[4])
     ff_tiles = hidden.shape[1] // hidden_width(tiles)
     ffn_count = 2 * ff_tiles
     count = ffn_count + KERNEL
@@ -1120,6 +1133,7 @@
         pl.when(t == 0)(lambda: load_lower.start())
         pl.when(t == 2)(lambda: load_pre.start())
         pl.when(t == 3)(lambda: load_ext.start())
+        pl.when(t == 4)(lambda: load_conv.start())
         pl.when(t == ffn_count)(lambda: each_load(0, lambda copy: copy.start()))
         chunk = t + 1
 
@@ -1135,6 +1149,7 @@
         def _():
             load_ext.wait()
             load_pre.wait()
+            load_conv.wait()
 
         rest = t - (count - 1)
 
@@ -1172,7 +1187,7 @@
     rows = group * rows_here
     return pl.pallas_call(
         functools.partial(reduce_kernel, steps),
-        in_specs=[pl.BlockSpec(memory_space=pltpu.SMEM), anywhere, anywhere, anywhere, anywhere, whole] + [anywhere] * 5 + [whole],
+        in_specs=[pl.BlockSpec(memory_space=pltpu.SMEM), anywhere, anywhere, anywhere, anywhere, whole] + [anywhere] * 6,
         out_specs=[anywhere] * 4 + [whole, anywhere, anywhere],
         out_shape=[
             jax.ShapeDtypeStruct(pre.shape, jnp.bfloat16),
@@ -1212,8 +1227,9 @@
             dma((RING, 3)), dma((RING, 3)), dma((RING, 3, 2)), dma((RING, 3, 2)), dma((RING, 2)), dma((RING, 2)),
             dma((RING, 2)), dma((RING, 2)), dma((RING,)), dma((RING,)), dma((2,)),
         ]
-        + [dma((4,)), dma((RING,)), dma((2, 4)), dma((2,)), dma((5,)), dma((5,))]
-        + [dma((steps - EARLY, 2)), dma((steps - EARLY, 2))],
+        + [dma((5,)), dma((RING,)), dma((2, 4)), dma((2,)), dma((5,)), dma((5,))]
+        + [dma((steps - EARLY, 2)), dma((steps - EARLY, 2))]
+        + [pltpu.VMEM(conv_w.shape, jnp.bfloat16)],
         compiler_params=pltpu.CompilerParams(
             vmem_limit_bytes=VMEM_BYTES, collective_id=1, has_side_effects=True
         ),

time: 242 us -> 239 us (0.988)
  Pallas kernels: 230 us -> 227 us
    pallas_call x1, Pallas kernels: 96.1 us -> 93.2 us  [blocks_halo(): pl.pallas_call(functools.partial(block_halo_kernel, count), grid=(count +...]
where the time goes in v5:
time: 239 us; the launch traced here: 238 us
  Pallas kernels  227 us (95%)
  local copies, waits for them, and re-layouts  9.66 us (4%)
    pallas_call x1, Pallas kernels, reduce_all(): pl.pallas_call(functools.partial(reduce_kernel, steps), in_specs=[pl.Bloc...  123 us
    pallas_call x1, Pallas kernels, blocks_halo(): pl.pallas_call(functools.partial(block_halo_kernel, count), grid=(count +...  93.2 us
    pallas_call x1, Pallas kernels, widened(): pl.pallas_call(widen_kernel, grid=(taps,), in_specs=specs, out_specs=spec...  10.8 us
    unnamed x6, local copies, waits for them, and re-layouts  8.13 us

profile of v5, /device:TPU:0, one launch (start us, length us, event | category | flops | bytes accessed | tf_op | source)
XLA Modules:
  0.0 238.5 jit_solution(1385096124229594714)
XLA Ops:
  0.7 1.3 compare_convert_fusion.refs_0_
  2.0 93.2 %block.1 = (bf16[32,128,512]{2,1,0:T(8,128)(2,1)}, bf16[32,384,512]{2,1,0:T(8,128)(2,1)}, bf16[32,128,512]{2,1,0:T(8,128)(2,1)}, bf16[32,128,512]{2,1,0:T(8,128)...) custom-call(f32[3,32]{1,0:T(4,128)} %compare_convert_fusion.refs_0_,, ...), custom_call_target="tpu_custom_call" | custom-call | tf_op jit(solution)/shard_map/block/pallas_call | solution.py:620
  95.1 122.8 %reduce.1 = (bf16[32,128,512]{2,1,0:T(8,128)(2,1)}, bf16[512,2048]{1,0:T(8,128)(2,1)}, bf16[2048,512]{1,0:T(8,128)(2,1)}, bf16[9,512,512]{2,1,0:T(8,128)(2,1)}, ...) custom-call(f32[3,32]{1,0:T(4,128)} %compare_convert_fusion.refs_0_, ...), custom_call_target="tpu_custom_call" | custom-call | tf_op jit(solution)/shard_map/reduce/pallas_call | solution.py:1188
  218.0 0.7 slice_bitcast_fusion
  218.7 1.5 fusion
  220.2 0.6 copy.25
  220.8 10.8 %tail.1 = (f32[512,2048]{1,0:T(8,128)}, f32[2048,512]{1,0:T(8,128)}, f32[9,512,512]{2,1,0:T(8,128)}) custom-call(bf16[512,2048]{1,0:T(8,128)(2,1)} %get-tuple-element.43.refs_0_, bf16[2048,512]{1,0:T(8,128)(2,1)} %get-tuple-element.44.refs_1_, bf16[9,512,512]{2,1,0:T(8,128)(2,1)} %get-tuple-element.45.refs_2_), custom_call_target="tpu_custom_call" | custom-call | tf_op jit(solution)/shard_map/tail/pallas_call | solution.py:1255
  231.7 0.0 copy-start
  231.7 4.8 %copy.28 = bf16[32,128,512]{2,1,0:T(8,128)(2,1)} copy(bf16[32,128,512]{2,1,0:T(8,128)(2,1)} %get-tuple-element.68) | data formatting | bytes 8388608
  236.5 0.0 copy-done
  236.5 2.0 copy.29
  (1 shorter events, 0.0 us)
Async XLA Ops:
  231.7 4.8 %copy-start = (bf16[32,128,512]{2,1,0:T(8,128)(2,1)S(1)}, bf16[32,128,512]{2,1,0:T(8,128)(2,1)}, u32[]{:S(2)}) copy-start(bf16[32,128,512]{2,1,0:T(8,128)(2,1)} %get-tuple-element.69) | copy-start | bytes 12582916
